TPU v7x, 32 devices: a whole 2x2x4 slice. The times are simulated.
32 devices in a mesh: chan: 16 (over z, y, core), tm: 2 (over x).
Axes of the slice: x: 2, y: 2, z: 4, core: 2. Of those that a mesh axis runs over, the one named last changes fastest.
Arguments:
- records: bfloat16 [6, 2048, 2048], P('tm', None, 'chan'), may hold values from -600 to 600
- band_taps: float32 [64], replicated, may hold values from -0.75 to 0.75
- white_taps: float32 [16, 2048], P(None, 'chan'), may hold values from -1.5 to 1.5
- live_mask: int32 [2048], P('chan'), may hold values 0 or 1
- partners: int32 [6, 16], P(None, 'chan'), may hold values from 0 to 15, as said below
Outputs:
- correlations: float32 [6, 32, 2048, 128], P(None, 'tm', 'chan')
Inputs may be any that keep to these rules, and one draw needn't show every extreme that they name: In each round blocks are matched in pairs: partners[r, b] differs from b, partners[r, partners[r, b]] = b, and partners[r, b] - b equals d or -d modulo 16, with the same d in the finite set (1, 2, 4) for all blocks of the round. Over all rounds every block b is matched with b + 1, b - 1, b + 2, b - 2, b + 4 and b - 4 modulo 16, each once.
All inputs are finite; a program needn't handle non-finite values. No bound on the sum of `live_mask` on one device may be relied on, other than what follows from the above.
Results may differ from a plain program's by a relative error of at most 0.0058.
Values may be sent and summed in bfloat16 or wider, within the bound.
A program may use at most 64 MiB of HBM per device.

v0:
```python
import math

import jax
import jax.numpy as jnp
from jax import lax
from jax.sharding import PartitionSpec as P

NB = 128
SEG = 6
LAGS = 32


def shifted(value, axis, steps):
    count = lax.axis_size(axis)
    pairs = [(source, (source + steps) % count) for source in range(count)]
    return lax.ppermute(value, axis, pairs)


def bin_numbers(samples, bin_count):
    return samples // 64 + samples // (4 * bin_count) * jnp.arange(bin_count, dtype=jnp.int32)


def rotation(products, samples):
    angles = jnp.mod(products, samples).astype(jnp.float32) * (2.0 * math.pi / samples)
    return (jnp.cos(angles), jnp.sin(angles))


def dft_table(samples, bin_index):
    sample_index = jnp.arange(samples, dtype=jnp.int32)
    cos_part, sin_part = rotation(sample_index[:, None] * bin_index[None, :], samples)
    return jnp.concatenate([cos_part, -sin_part], axis=1).astype(jnp.bfloat16)


def responses(band_taps, white_taps, bin_index, samples):
    highest = lax.Precision.HIGHEST
    band_cos, band_sin = rotation(
        jnp.arange(band_taps.shape[0], dtype=jnp.int32)[:, None] * bin_index[None, :], samples
    )
    white_cos, white_sin = rotation(
        jnp.arange(white_taps.shape[0], dtype=jnp.int32)[:, None] * bin_index[None, :], samples
    )
    band_real = jnp.dot(band_taps, band_cos, precision=highest)
    band_imag = -jnp.dot(band_taps, band_sin, precision=highest)
    white_real = jnp.dot(white_taps.T, white_cos, precision=highest)
    white_imag = -jnp.dot(white_taps.T, white_sin, precision=highest)
    resp_real = white_real * band_real[None, :] - white_imag * band_imag[None, :]
    resp_imag = white_real * band_imag[None, :] + white_imag * band_real[None, :]
    return (resp_real, resp_imag)


def filtered(raw_spec, resp_real, resp_imag, live_values):
    bin_count = resp_real.shape[1]
    spec_real = raw_spec[..., :bin_count]
    spec_imag = raw_spec[..., bin_count:]
    real_resp = resp_real[:, None, :]
    imag_resp = resp_imag[:, None, :]
    out_real = (real_resp * spec_real - imag_resp * spec_imag) * live_values[:, None, None]
    out_imag = (real_resp * spec_imag + imag_resp * spec_real) * live_values[:, None, None]
    return jnp.concatenate([out_real, out_imag], axis=2).astype(jnp.bfloat16)


def inverse_norms(flat_rows):
    values = flat_rows.astype(jnp.float32)
    mean_square = jnp.sum(values * values, axis=-1) / (SEG * NB)
    return lax.rsqrt(mean_square + 1e-06)


def turned_rows(own_block, lag_values, bin_index, samples):
    lag_cos, lag_sin = rotation(lag_values[:, None] * bin_index[None, :], samples)
    values = own_block.astype(jnp.float32).reshape(own_block.shape[0], SEG, 2, NB)
    part_real = values[:, :, 0, :][None]
    part_imag = values[:, :, 1, :][None]
    cos_factor = lag_cos[:, None, None, :]
    sin_factor = lag_sin[:, None, None, :]
    new_real = part_real * cos_factor - part_imag * sin_factor
    new_imag = part_real * sin_factor + part_imag * cos_factor
    stacked = jnp.stack([new_real, new_imag], axis=3)
    return stacked.astype(jnp.bfloat16).reshape(lag_values.shape[0] * own_block.shape[0], -1)


def tile_sums(turned, chosen, own_scale, part_scale, lag_count):
    rounds, row_count, inner_size = chosen.shape
    flat_rows = chosen.reshape(rounds * row_count, inner_size)
    tile_totals = lax.dot_general(
        turned, flat_rows, (((1,), (1,)), ((), ())), preferred_element_type=jnp.float32
    )
    tile_totals = tile_totals.reshape(lag_count, row_count, rounds, row_count)
    scaled = (
        tile_totals
        * own_scale[None, :, None, None]
        * part_scale[None, None, :, :]
        * (1.0 / math.sqrt(SEG * NB))
    )
    return jnp.transpose(scaled, (2, 0, 1, 3))


def local(records, band_taps, white_taps, live_mask, partners):
    samples = records.shape[1]
    channels = records.shape[2]
    bin_index = bin_numbers(samples, NB)
    transform = dft_table(samples, bin_index)
    resp_real, resp_imag = responses(band_taps, white_taps, bin_index, samples)
    live_values = live_mask.astype(jnp.float32)
    raw_spec = jnp.einsum(
        "stc,tf->csf",
        lax.all_gather(records, "tm", axis=0, tiled=True),
        transform,
        preferred_element_type=jnp.float32,
    )
    spectra = filtered(raw_spec, resp_real, resp_imag, live_values)
    own_block = spectra.reshape(channels, -1)
    my_block = lax.axis_index("chan")
    block_count = lax.axis_size("chan")
    offset_list = (-4, -2, -1, 1, 2, 4)
    pieces = {}
    for offset in (1, 2, 4, -1, -2, -4):
        pieces[offset] = shifted(own_block, "chan", -offset)
    window = jnp.stack([pieces[offset] for offset in offset_list])
    delta = jnp.mod(partners[:, 0] - my_block + block_count // 2, block_count) - block_count // 2
    slot_index = jnp.zeros_like(delta)
    for position, offset in enumerate(offset_list):
        slot_index = slot_index + position * (delta == offset).astype(jnp.int32)
    chosen = jnp.take(window, slot_index, axis=0)
    own_scale = inverse_norms(own_block)
    part_scale = inverse_norms(chosen)
    lag_count = LAGS // lax.axis_size("tm")
    lag_first = lax.axis_index("tm") * lag_count
    lag_values = 3 * (lag_first + jnp.arange(lag_count, dtype=jnp.int32) - LAGS // 2)
    turned = turned_rows(own_block, lag_values, bin_index, samples)
    return tile_sums(turned, chosen, own_scale, part_scale, lag_count)


def solution(mesh):
    return jax.shard_map(
        local,
        mesh=mesh,
        in_specs=(P("tm", None, "chan"), P(), P(None, "chan"), P("chan"), P(None, "chan")),
        out_specs=P(None, "tm", "chan", None),
        check_vma=False,
    )
```

profile of v0, /device:TPU:0, one launch (start us, length us, event | category | flops | bytes accessed | tf_op | source)
XLA Modules:
  0.0 143.6 jit_solution(6324323348787605801)
XLA Ops:
  6.5 0.7 all-gather.2.cloned.1.call-update
  7.3 0.7 convert_element_type.73
  7.9 0.7 and_bitcast_fusion
  8.6 0.9 convolution_bitcast_fusion.2
  9.6 0.9 fusion.5
  10.7 0.3 convolution_negate_fusion
  11.0 0.3 subtract_bitcast_fusion
  11.4 4.9 %cosine_convert_fusion = (bf16[2048,128]{0,1:T(8,128)(2,1)S(1)}, bf16[2048,128]{0,1:T(8,128)(2,1)S(1)}) fusion(s32[128]{0:T(128)S(1)} %multiply_add_fusion), kind=kLoop, calls=%fused_computation.25 | loop fusion | flops 4456448 | bytes 1049088 | tf_op jit(solution)/shard_map/convert.3
  16.2 40.4 %all-gather.2.cloned.1.call-done = bf16[6,2048,128]{2,1,0:T(8,128)(2,1)} async-done(((bf16[3,2048,128]{2,1,0:T(8,128)(2,1)}), bf16[6,2048,128]{2,1,0:T(8,128)(2,1)}) %all-gather.2.cloned.1.call-update) | async-done | bytes 3145744 | tf_op jit(solution)/shard_map/all_gather | solution.py:106
  56.7 2.9 %convolution_bitcast_fusion = f32[128,6,256]{0,2,1:T(8,128)S(1)} fusion(bf16[6,2048,128]{2,1,0:T(8,128)(2,1)} %all-gather.2.cloned.1.call-done, bf16[2048,128]{0,1:T(8,128)(2,1)S(1)} %get-tuple-element.20, bf16[2048,128]{0,1:T(8,128)(2,1)S(1)} %get-tuple-element.19), kind=kOutput, calls=%fused_computation.13 | convolution fusion | flops 807403520 | bytes 4980736 | tf_op jit(solution)/shard_map/stc,tf->csf/dot_general | solution.py:104
  59.7 0.2 multiply_reduce_fusion.1
  60.1 1.5 %collective-permute-start = (bf16[128,1536]{1,0:T(8,128)(2,1)S(1)}, bf16[128,1536]{1,0:T(8,128)(2,1)}, u32[]{:S(2)}, u32[]{:S(2)}) collective-permute-start(bf16[128,1536]{1,0:T(8,128)(2,1)S(1)} %copy.20), channel_id=1, source_target_pairs={{0,8},{2,10},{4,12},{6,14},{8,16},{10,18},{12,20},{14,22},{16,24},... | collective-permute-start | bytes 1179656 | tf_op jit(solution)/shard_map/ppermute | solution.py:16
  61.5 1.5 %collective-permute-start.1 = (bf16[128,1536]{1,0:T(8,128)(2,1)S(1)}, bf16[128,1536]{1,0:T(8,128)(2,1)S(1)}, u32[]{:S(2)}, u32[]{:S(2)}) collective-permute-start(bf16[128,1536]{1,0:T(8,128)(2,1)S(1)} %copy.20), channel_id=1, source_target_pairs={{0,4},{2,6},{4,8},{6,10},{8,12},{10,14},{12,16},{14,18},{16,20},{1... | collective-permute-start | bytes 1179656 | tf_op jit(solution)/shard_map/ppermute | solution.py:16
  63.0 4.4 %collective-permute-start.3 = (bf16[128,1536]{1,0:T(8,128)(2,1)S(1)}, bf16[128,1536]{1,0:T(8,128)(2,1)S(1)}, u32[]{:S(2)}, u32[]{:S(2)}) collective-permute-start(bf16[128,1536]{1,0:T(8,128)(2,1)S(1)} %copy.20), channel_id=1, source_target_pairs={{0,30},{2,0},{4,2},{6,4},{8,6},{10,8},{12,10},{14,12},{16,14},{18,... | collective-permute-start | bytes 1179656 | tf_op jit(solution)/shard_map/ppermute | solution.py:16
  67.5 0.6 collective-permute-start.4
  68.2 0.2 copy.18
  68.4 0.2 copy.19
  68.6 13.2 %subtract_convert_fusion = (bf16[16,128,6,1,128]{4,3,2,1,0:T(2,128)(2,1)S(1)}, bf16[16,128,6,1,128]{4,3,2,1,0:T(2,128)(2,1)S(1)}) fusion(f32[16,128]{1,0:T(8,128)S(1)} %get-tuple-element.18, f32[128,6,128]{2,1,0:T(8,128)S(1)} %copy.19, f32[16,128]{1,0:T(8,128)S(1)} %get-tuple-element.17, f32[128,6,128]{2,1,0:T(8,128)S(1)} %copy.18), kind=kLoop, calls=%fused_computation.6 | loop fusion | flops 12582912 | bytes 7094272 | tf_op jit(solution)/shard_map/convert.1
  81.9 15.4 %pad_maximum_fusion = bf16[16,128,6,2,128]{4,3,2,1,0:T(2,128)(2,1)} fusion(bf16[16,128,6,1,128]{4,3,2,1,0:T(2,128)(2,1)S(1)} %get-tuple-element.10, bf16[16,128,6,1,128]{4,3,2,1,0:T(2,128)(2,1)S(1)} %get-tuple-element.9), kind=kLoop, calls=%fused_computation.1 | loop fusion | flops 12582912 | bytes 12582912 | tf_op jit(solution)/shard_map/stack | solution.py:77
  97.2 14.4 %reshape.152 = bf16[16,128,1536,1]{2,1,0,3:T(8,128)(2,1)} reshape(bf16[16,128,6,2,128]{4,3,2,1,0:T(2,128)(2,1)} %pad_maximum_fusion) | data formatting | bytes 12582912 | tf_op jit(solution)/shard_map/convert_element_type | solution.py:78
  111.6 0.7 collective-permute-start.5
  112.3 1.8 %bitcast_dynamic-update-slice_fusion.5 = bf16[6,128,1536]{2,1,0:T(8,128)(2,1)} fusion(bf16[128,1536]{1,0:T(8,128)(2,1)} %collective-permute-done), kind=kLoop, calls=%fused_computation.38 | loop fusion | bytes 786432
  114.1 0.8 bitcast_dynamic-update-slice_fusion.4
  114.9 0.8 bitcast_dynamic-update-slice_fusion.3
  115.6 0.8 bitcast_dynamic-update-slice_fusion.2
  116.4 0.8 bitcast_dynamic-update-slice_fusion.1
  117.2 5.1 %collective-permute-done.5 = bf16[128,1536]{1,0:T(8,128)(2,1)S(1)} collective-permute-done((bf16[128,1536]{1,0:T(8,128)(2,1)S(1)}, bf16[128,1536]{1,0:T(8,128)(2,1)S(1)}, u32[]{:S(2)}, u32[]{:S(2)}) %collective-permute-start.5) | collective-permute-done | bytes 393248 | tf_op jit(solution)/shard_map/ppermute | solution.py:16
  122.3 0.8 bitcast_dynamic-update-slice_fusion
  123.1 2.4 %gather_fusion = bf16[6,128,1536]{2,1,0:T(8,128)(2,1)S(1)} fusion(bf16[6,128,1536]{2,1,0:T(8,128)(2,1)} %bitcast_dynamic-update-slice_fusion, s32[1024]{0:T(1024)S(1)} %pad_clamp_fusion), kind=kCustom, calls=%fused_computation | custom fusion | bytes 4718616 | tf_op jit(solution)/shard_map/jit(_take)/gather | solution.py:123
  125.4 0.8 multiply_reduce_fusion
  126.2 7.4 %multiply_bitcast_fusion = f32[6,16,128,128]{3,2,0,1:T(8,128)S(1)} fusion(f32[6,128]{1,0:T(8,128)S(1)} %add_rsqrt_fusion, f32[128]{0:T(128)S(1)} %add_rsqrt_fusion.1, bf16[16,128,1536,1]{2,1,0,3:T(8,128)(2,1)} %reshape.152, bf16[6,128,1536]{2,1,0:T(8,128)(2,1)S(1)} %gather_fusion, pred[6]{0:T(512)(128)(4,1)S(1)} %get-tuple-element.7), kind=kOutput, calls=%fused_computation.4 | convolution fusion | flops 4837736448 | bytes 14945798 | tf_op jit(solution)/shard_map/dot_general | solution.py:84
  133.6 3.1 %copy.26 = f32[6,16,128,128]{3,2,1,0:T(8,128)} copy(f32[6,16,128,128]{3,2,0,1:T(8,128)S(1)} %multiply_bitcast_fusion) | data formatting | bytes 12582912 | tf_op jit(solution)/shard_map/mul | solution.py:89
  (19 shorter events, 0.6 us)
Async XLA Ops:
  6.5 4.1 %copy-start = (f32[16,128]{1,0:T(8,128)S(1)}, f32[16,128]{1,0:T(8,128)}, u32[]{:S(2)}) copy-start(f32[16,128]{1,0:T(8,128)} %param.7) | copy-start | bytes 24580
  6.5 50.1 %all-gather.2.cloned.1.call-start = ((), (), s32[]{:S(2)}) async-start(), calls=%async_computation | async-start | bytes 4718592 | tf_op jit(solution)/shard_map/all_gather | solution.py:106
  60.1 51.6 %collective-permute-start = (bf16[128,1536]{1,0:T(8,128)(2,1)S(1)}, bf16[128,1536]{1,0:T(8,128)(2,1)}, u32[]{:S(2)}, u32[]{:S(2)}) collective-permute-start(bf16[128,1536]{1,0:T(8,128)(2,1)S(1)} %copy.20), channel_id=1, source_target_pairs={{0,8},{2,10},{4,12},{6,14},{8,16},{10,18},{12,20},{14,22},{16,24},... | collective-permute-start | bytes 1179656 | tf_op jit(solution)/shard_map/ppermute | solution.py:16
  61.5 52.5 %collective-permute-start.1 = (bf16[128,1536]{1,0:T(8,128)(2,1)S(1)}, bf16[128,1536]{1,0:T(8,128)(2,1)S(1)}, u32[]{:S(2)}, u32[]{:S(2)}) collective-permute-start(bf16[128,1536]{1,0:T(8,128)(2,1)S(1)} %copy.20), channel_id=1, source_target_pairs={{0,4},{2,6},{4,8},{6,10},{8,12},{10,14},{12,16},{14,18},{16,20},{1... | collective-permute-start | bytes 1179656 | tf_op jit(solution)/shard_map/ppermute | solution.py:16
  63.0 51.8 %collective-permute-start.2 = (bf16[128,1536]{1,0:T(8,128)(2,1)S(1)}, bf16[128,1536]{1,0:T(8,128)(2,1)S(1)}, u32[]{:S(2)}, u32[]{:S(2)}) collective-permute-start(bf16[128,1536]{1,0:T(8,128)(2,1)S(1)} %copy.20), channel_id=1, source_target_pairs={{0,2},{2,4},{4,6},{6,8},{8,10},{10,12},{12,14},{14,16},{16,18},{18... | collective-permute-start | bytes 1179656 | tf_op jit(solution)/shard_map/ppermute | solution.py:16
  63.0 52.6 %collective-permute-start.3 = (bf16[128,1536]{1,0:T(8,128)(2,1)S(1)}, bf16[128,1536]{1,0:T(8,128)(2,1)S(1)}, u32[]{:S(2)}, u32[]{:S(2)}) collective-permute-start(bf16[128,1536]{1,0:T(8,128)(2,1)S(1)} %copy.20), channel_id=1, source_target_pairs={{0,30},{2,0},{4,2},{6,4},{8,6},{10,8},{12,10},{14,12},{16,14},{18,... | collective-permute-start | bytes 1179656 | tf_op jit(solution)/shard_map/ppermute | solution.py:16
  67.5 49.0 %collective-permute-start.4 = (bf16[128,1536]{1,0:T(8,128)(2,1)S(1)}, bf16[128,1536]{1,0:T(8,128)(2,1)S(1)}, u32[]{:S(2)}, u32[]{:S(2)}) collective-permute-start(bf16[128,1536]{1,0:T(8,128)(2,1)S(1)} %copy.20), channel_id=1, source_target_pairs={{0,28},{2,30},{4,0},{6,2},{8,4},{10,6},{12,8},{14,10},{16,12},{18,... | collective-permute-start | bytes 1179656 | tf_op jit(solution)/shard_map/ppermute | solution.py:16
  111.6 10.7 %collective-permute-start.5 = (bf16[128,1536]{1,0:T(8,128)(2,1)S(1)}, bf16[128,1536]{1,0:T(8,128)(2,1)S(1)}, u32[]{:S(2)}, u32[]{:S(2)}) collective-permute-start(bf16[128,1536]{1,0:T(8,128)(2,1)S(1)} %copy.20), channel_id=1, source_target_pairs={{0,24},{2,26},{4,28},{6,30},{8,0},{10,2},{12,4},{14,6},{16,8},{18,... | collective-permute-start | bytes 1179656 | tf_op jit(solution)/shard_map/ppermute | solution.py:16
Sparse Core Ops, SparseCore 0:
  8.9 47.7 all-gather.1
where the time goes:
time: 144 us
  waiting for transfers between devices  46.3 us (32%)
  other arithmetic  36.1 us (25%)
  local copies, waits for them, and re-layouts  26.2 us (18%)
  between operations  13.5 us (9%)
  matrix products  12.8 us (9%)
  starting transfers between devices  8.6 us (6%)
    all_gather x1, waiting for transfers between devices, local(): lax.all_gather(records, 'tm', axis=0, tiled=True)  40.4 us
    another operation x2, other arithmetic  18.1 us
    another operation x1, other arithmetic, turned_rows(): stacked = jnp.stack([new_real, new_imag], axis=3)  15.4 us
    convert_element_type x1, local copies, waits for them, and re-layouts, turned_rows(): stacked.astype(jnp.bfloat16)  14.4 us
    ppermute x6, starting transfers between devices, shifted(): return lax.ppermute(value, axis, pairs)  8.6 us
    dot_general x1, matrix products, tile_sums(): lax.dot_general(turned, flat_rows, (((1,), (1,)), ((), ())), preferred_el...  7.37 us
    ppermute x6, waiting for transfers between devices, shifted(): return lax.ppermute(value, axis, pairs)  5.14 us
    unnamed x7, local copies, waits for them, and re-layouts  4.86 us
  transfers between devices with their start and end apart: 7, of which 2 were waited for; matrix products, arithmetic and copies ran while one was open for 40% of the time, Pallas kernels for 0%

commit v1 on v0

v1 whole, which is shorter than its diff:
```python
import functools
import math

import jax
import jax.numpy as jnp
import numpy as np
from jax import lax
from jax.experimental import pallas as pl
from jax.experimental.pallas import tpu as pltpu
from jax.sharding import PartitionSpec as P

NB = 128
SEG = 6
LAGS = 32
ROUNDS = 6
GROUP = 4
MESH = pl.DeviceIdType.MESH
VMEM = pltpu.VMEM
SMEM = pltpu.SMEM
OFFSETS = (-4, -2, -1, 1, 2, 4)


def bin_numbers(samples):
    return samples // 64 + samples // (4 * NB) * np.arange(NB, dtype=np.int64)


def rotation(products, samples):
    angles = np.mod(products, samples) * (2.0 * math.pi / samples)
    return np.cos(angles), np.sin(angles)


def gather_kernel(
    count, segs,
    rec, table, band_cos, band_sin, white_cos, white_sin, band, white, live,
    win, own_t,
    own, send, recv_x, recv_w,
):
    me = lax.axis_index("chan")
    tm = lax.axis_index("tm")
    core = lax.rem(me, 2)
    side = lax.rem(me // 2, 2)
    up = lax.rem(me + 4, count)
    down = lax.rem(me + count - 4, count)
    sib = me + 1 - 2 * core
    across = me + 2 - 4 * side
    other = 1 - tm

    barrier = pltpu.get_barrier_semaphore()
    for peer in ((me, other), (up, tm), (down, tm), (across, tm), (sib, tm)):
        pl.semaphore_signal(barrier, inc=1, device_id=peer, device_id_type=MESH)

    def seg_at(i):
        return tm * segs + i if i < segs else other * segs + (i - segs)

    sends = []

    def start(src, dst, sem, peer):
        copy = pltpu.make_async_remote_copy(
            src_ref=src, dst_ref=dst, send_sem=send.at[len(sends)], recv_sem=sem,
            device_id=peer, device_id_type=MESH,
        )
        copy.start()
        sends.append(copy)

    def arrived(dst, sem):
        pltpu.make_async_remote_copy(
            src_ref=dst, dst_ref=dst, send_sem=send.at[0], recv_sem=sem,
            device_id=(me, other), device_id_type=MESH,
        ).wait_recv()

    def wait_win(slot, seg):
        arrived(win.at[slot, seg], recv_w.at[slot, seg])

    def spread(seg):
        for slot, peer in ((0, up), (5, down), (1 + 3 * side, across), (2 + core, sib)):
            start(own.at[seg], win.at[slot, seg], recv_w.at[slot, seg], (peer, tm))

    relay_src, relay_dst = 5 - 5 * side, 4 - 3 * side
    pass_src, pass_dst = 4 - 3 * core, 3 - core

    def relay(seg):
        wait_win(relay_src, seg)
        start(win.at[relay_src, seg], win.at[relay_dst, seg], recv_w.at[relay_dst, seg], (across, tm))

    def hand_on(seg):
        wait_win(pass_src, seg)
        start(win.at[pass_src, seg], win.at[pass_dst, seg], recv_w.at[pass_dst, seg], (sib, tm))

    taps = band[...]
    band_re = jnp.sum(band_cos[...] * taps, axis=1, keepdims=True)
    band_im = -jnp.sum(band_sin[...] * taps, axis=1, keepdims=True)
    highest = lax.Precision.HIGHEST
    white_re = jnp.dot(white_cos[...], white[...], precision=highest, preferred_element_type=jnp.float32)
    white_im = -jnp.dot(white_sin[...], white[...], precision=highest, preferred_element_type=jnp.float32)
    resp_re = white_re * band_re - white_im * band_im
    resp_im = white_re * band_im + white_im * band_re
    alive = live[...].astype(jnp.float32)

    period = table.shape[1]
    for i in range(segs):
        raw = jnp.zeros((2 * NB, rec.shape[2]), jnp.float32)
        for first in range(0, rec.shape[1], period):
            raw = raw + jnp.dot(
                table[...], rec[i, first:first + period, :], preferred_element_type=jnp.float32
            )
        raw_re, raw_im = raw[:NB], raw[NB:]
        seg = seg_at(i)
        own[seg, :NB, :] = ((resp_re * raw_re - resp_im * raw_im) * alive).astype(jnp.bfloat16)
        own[seg, NB:, :] = ((resp_re * raw_im + resp_im * raw_re) * alive).astype(jnp.bfloat16)
        if i == 0:
            pl.semaphore_wait(barrier, 5)
        start(own.at[seg], own.at[seg], recv_x.at[i], (me, other))
        spread(seg)

    for i in range(segs):
        seg = seg_at(segs + i)
        arrived(own.at[seg], recv_x.at[i])
        spread(seg)
        relay(seg_at(i))
        if i:
            hand_on(seg_at(i - 1))
    for i in range(segs, 2 * segs):
        relay(seg_at(i))
        hand_on(seg_at(i - 1))
        if i == segs:
            for s in range(2 * segs):
                for part in range(2):
                    rows = own[s, part * NB:(part + 1) * NB, :].astype(jnp.float32)
                    at = (2 * s + part) * NB
                    own_t[:, at:at + NB] = rows.T.astype(jnp.bfloat16)
    hand_on(seg_at(2 * segs - 1))

    for i in range(2 * segs):
        for slot in (5 * side, 1 + 3 * core, 2, 3):
            wait_win(slot, seg_at(i))
    for copy in sends:
        copy.wait_send()


def correlate_kernel(count, place, partners, lag_table, own_t, win, out, wide, turned, scale_own, scale_win):
    step = pl.program_id(0)
    me = place[0]
    lag_first = place[1] * (LAGS // 2) + step * GROUP
    channels = own_t.shape[0]
    inner = own_t.shape[1]

    @pl.when(step == 0)
    def _():
        values = own_t[...].astype(jnp.float32)
        wide[...] = values
        mean_square = jnp.sum(values * values, axis=1, keepdims=True) / (SEG * NB)
        scale_own[...] = lax.rsqrt(mean_square + 1e-06) * (1.0 / math.sqrt(SEG * NB))
        for slot in range(len(OFFSETS)):
            rows = win[slot].astype(jnp.float32)
            total = jnp.sum(jnp.sum(rows * rows, axis=0), axis=0, keepdims=True) / (SEG * NB)
            scale_win[slot] = lax.rsqrt(total + 1e-06)

    for l in range(GROUP):
        pair = lag_table[lag_first + l]
        cos, sin = pair[0:1], pair[1:2]
        rows = slice(l * channels, (l + 1) * channels)
        for s in range(SEG):
            at = 2 * s * NB
            re, im = wide[:, at:at + NB], wide[:, at + NB:at + 2 * NB]
            turned[rows, at:at + NB] = (re * cos - im * sin).astype(jnp.bfloat16)
            turned[rows, at + NB:at + 2 * NB] = (re * sin + im * cos).astype(jnp.bfloat16)

    def slot_of(r):
        delta = lax.rem(partners[r, 0] - me + count + count // 2, count) - count // 2
        slot = jnp.int32(0)
        for position, offset in enumerate(OFFSETS):
            slot = slot + jnp.where(delta == offset, position, 0)
        return slot

    own_scale = scale_own[...]
    for r in range(0, ROUNDS, 2):
        slots = (slot_of(r), slot_of(r + 1))
        chosen = jnp.concatenate([win[s].reshape(inner, channels) for s in slots], axis=1)
        sums = jnp.dot(turned[...], chosen, preferred_element_type=jnp.float32)
        for k in range(2):
            part = sums[:, k * channels:(k + 1) * channels].reshape(GROUP, channels, channels)
            out[r + k] = part * own_scale[None] * scale_win[slots[k]][None]


def local(records, band_taps, white_taps, live_mask, partners):
    segs, samples, channels = records.shape
    count = lax.axis_size("chan")
    inner = SEG * 2 * NB
    lag_count = LAGS // lax.axis_size("tm")
    bins = bin_numbers(samples)
    period = samples // math.gcd(samples, math.gcd(int(bins[0]), int(bins[1] - bins[0])))
    cos, sin = rotation(bins[:, None] * np.arange(period)[None, :], samples)
    table = np.concatenate([cos, -sin], axis=0).astype(np.float32).astype(jnp.bfloat16)
    band_cos, band_sin = rotation(bins[:, None] * np.arange(band_taps.shape[0])[None, :], samples)
    white_cos, white_sin = rotation(bins[:, None] * np.arange(white_taps.shape[0])[None, :], samples)
    f32 = lambda a: jnp.asarray(a.astype(np.float32))

    vmem = pl.BlockSpec(memory_space=VMEM)
    win, own_t = pl.pallas_call(
        functools.partial(gather_kernel, count, segs),
        out_shape=(
            jax.ShapeDtypeStruct((6, SEG, 2 * NB, channels), jnp.bfloat16),
            jax.ShapeDtypeStruct((channels, inner), jnp.bfloat16),
        ),
        in_specs=[vmem] * 9,
        out_specs=(pl.BlockSpec(memory_space=pl.ANY), vmem),
        scratch_shapes=[
            VMEM((SEG, 2 * NB, channels), jnp.bfloat16),
            pltpu.SemaphoreType.DMA((segs + 6 * SEG,)),
            pltpu.SemaphoreType.DMA((segs,)),
            pltpu.SemaphoreType.DMA((6, SEG)),
        ],
        compiler_params=pltpu.CompilerParams(
            collective_id=0, has_side_effects=True, vmem_limit_bytes=32 * 1024 * 1024
        ),
        name="spectra_gather",
    )(
        records, jnp.asarray(table), f32(band_cos), f32(band_sin), f32(white_cos), f32(white_sin),
        band_taps.reshape(1, -1), white_taps, live_mask.reshape(1, -1),
    )

    lags = 3 * (np.arange(LAGS) - LAGS // 2)
    lag_table = np.stack(rotation(lags[:, None] * bins[None, :], samples), axis=1)
    place = jnp.stack([lax.axis_index("chan"), lax.axis_index("tm")]).astype(jnp.int32)
    whole = lambda *shape: pl.BlockSpec(shape, lambda i: (0,) * len(shape))
    smem = pl.BlockSpec(memory_space=SMEM)
    return pl.pallas_call(
        functools.partial(correlate_kernel, count),
        grid=(lag_count // GROUP,),
        out_shape=jax.ShapeDtypeStruct((ROUNDS, lag_count, channels, channels), jnp.float32),
        in_specs=[
            smem, smem, whole(LAGS, 2, NB), whole(channels, inner),
            whole(6, SEG, 2 * NB, channels),
        ],
        out_specs=pl.BlockSpec((ROUNDS, GROUP, channels, channels), lambda i: (0, i, 0, 0)),
        scratch_shapes=[
            VMEM((channels, inner), jnp.float32),
            VMEM((GROUP * channels, inner), jnp.bfloat16),
            VMEM((channels, 1), jnp.float32),
            VMEM((6, 1, channels), jnp.float32),
        ],
        compiler_params=pltpu.CompilerParams(vmem_limit_bytes=48 * 1024 * 1024),
        name="correlate",
    )(place, partners, f32(lag_table), own_t, win)


def solution(mesh):
    return jax.shard_map(
        local,
        mesh=mesh,
        in_specs=(P("tm", None, "chan"), P(), P(None, "chan"), P("chan"), P(None, "chan")),
        out_specs=P(None, "tm", "chan", None),
        check_vma=False,
    )
```

time: 144 us -> 46 us (0.32)
  waiting for transfers between devices: 46.3 us -> 0 us
  Pallas kernels: 0 us -> 36.2 us
  other arithmetic: 36.1 us -> 0.07 us
  local copies, waits for them, and re-layouts: 26.2 us -> 9.21 us
  between operations: 13.5 us -> 0.03 us
  matrix products: 12.8 us -> 0 us
  starting transfers between devices: 8.6 us -> 0 us
    all_gather x1 -> x0, waiting for transfers between devices: 40.4 us -> none  [local(): lax.all_gather(records, 'tm', axis=0, tiled=True)]
    pallas_call x0 -> x2, Pallas kernels: none -> 36.2 us  [the longest x1 27.6 us: local(): pl.pallas_call(functools.partial(gather_kernel, count, segs), out_shape=(...]
    another operation x3 -> x1, other arithmetic: 33.5 us -> 0.07 us  [local(): jnp.stack([lax.axis_index('chan'), lax.axis_index('tm')]).astype(jnp.int32)]
    convert_element_type x2 -> x0, local copies, waits for them, and re-layouts: 14.6 us -> none  [the longest x1 14.4 us: turned_rows(): stacked.astype(jnp.bfloat16)]
    dot_general x6 -> x0, matrix products: 12.8 us -> none  [the longest x1 7.37 us: tile_sums(): lax.dot_general(turned, flat_rows, (((1,), (1,)), ((), ())), preferred_el...]
    ppermute x6 -> x0, starting transfers between devices: 8.6 us -> none  [shifted(): return lax.ppermute(value, axis, pairs)]
    ppermute x6 -> x0, waiting for transfers between devices: 5.14 us -> none  [shifted(): return lax.ppermute(value, axis, pairs)]
    unnamed x7 -> x21, local copies, waits for them, and re-layouts: 4.86 us -> 9.21 us
  transfers between devices with their start and end apart: 7 -> 0, of which waited for: 2 -> 0; matrix products, arithmetic and copies ran while one was open for 40% -> 0% of each run, Pallas kernels for 0% -> 0%
where the time goes in v1:
time: 46 us; the launch traced here: 45.5 us
  Pallas kernels  36.2 us (79%)
  local copies, waits for them, and re-layouts  9.21 us (20%)
    pallas_call x1, Pallas kernels, local(): pl.pallas_call(functools.partial(gather_kernel, count, segs), out_shape=(...  27.6 us
    unnamed x21, local copies, waits for them, and re-layouts  9.21 us
    pallas_call x1, Pallas kernels, local(): pl.pallas_call(functools.partial(correlate_kernel, count), grid=(lag_coun...  8.56 us

profile of v1, /device:TPU:0, one launch (start us, length us, event | category | flops | bytes accessed | tf_op | source)
XLA Modules:
  0.0 45.5 jit_solution(12899469874961496501)
XLA Ops:
  0.0 0.1 pad_add_fusion.place
  0.1 0.7 %copy.12.partners = s32[6,1]{1,0:T(8,128)S(1)} copy(s32[6,1]{0,1:T(1,128)} %param.15) | data formatting | bytes 48 | tf_op args[4]
  0.8 0.0 copy-start
  0.8 1.4 %copy-done = bf16[3,2048,128]{2,1,0:T(8,128)(2,1)S(1)} copy-done((bf16[3,2048,128]{2,1,0:T(8,128)(2,1)S(1)}, bf16[3,2048,128]{2,1,0:T(8,128)(2,1)}, u32[]{:S(2)}) %copy-start) | copy-done | bytes 1572888
  2.2 0.0 copy-start.1
  2.2 0.9 %copy-done.1 = bf16[256,512]{1,0:T(8,128)(2,1)S(1)} copy-done((bf16[256,512]{1,0:T(8,128)(2,1)S(1)}, bf16[256,512]{1,0:T(8,128)(2,1)}, u32[]{:S(2)}) %copy-start.1) | copy-done | bytes 262168
  3.2 0.0 copy-start.2
  3.2 0.8 %copy-done.2 = f32[128,16]{1,0:T(8,128)S(1)} copy-done((f32[128,16]{1,0:T(8,128)S(1)}, f32[128,16]{1,0:T(8,128)}, u32[]{:S(2)}) %copy-start.2) | copy-done | bytes 8216
  4.0 0.0 copy-start.3
  4.0 0.8 %copy-done.3 = f32[128,16]{1,0:T(8,128)S(1)} copy-done((f32[128,16]{1,0:T(8,128)S(1)}, f32[128,16]{1,0:T(8,128)}, u32[]{:S(2)}) %copy-start.3) | copy-done | bytes 8216
  4.9 0.0 copy-start.4
  4.9 0.8 %copy-done.4 = f32[128,64]{1,0:T(8,128)S(1)} copy-done((f32[128,64]{1,0:T(8,128)S(1)}, f32[128,64]{1,0:T(8,128)}, u32[]{:S(2)}) %copy-start.4) | copy-done | bytes 32792
  5.7 0.0 copy-start.5
  5.7 0.8 %copy-done.5 = f32[128,64]{1,0:T(8,128)S(1)} copy-done((f32[128,64]{1,0:T(8,128)S(1)}, f32[128,64]{1,0:T(8,128)}, u32[]{:S(2)}) %copy-start.5) | copy-done | bytes 32792
  6.5 0.0 copy-start.7
  6.5 0.7 %copy-done.7 = f32[16,128]{1,0:T(8,128)S(1)} copy-done((f32[16,128]{1,0:T(8,128)S(1)}, f32[16,128]{1,0:T(8,128)}, u32[]{:S(2)}) %copy-start.7) | copy-done | bytes 8216
  7.2 0.0 copy-start.8
  7.2 0.7 %copy-done.8 = f32[64]{0:T(128)S(1)} copy-done((f32[64]{0:T(128)S(1)}, f32[64]{0:T(128)}, u32[]{:S(2)}) %copy-start.8) | copy-done | bytes 280
  7.9 0.0 copy-start.9
  7.9 0.7 %copy-done.9 = s32[128]{0:T(128)S(1)} copy-done((s32[128]{0:T(128)S(1)}, s32[128]{0:T(128)}, u32[]{:S(2)}) %copy-start.9) | copy-done | bytes 536
  8.5 27.6 %spectra_gather.1 = (bf16[6,6,256,128]{3,2,1,0:T(8,128)(2,1)S(1)}, bf16[128,1536]{1,0:T(8,128)(2,1)S(1)}) custom-call(bf16[3,2048,128]{2,1,0:T(8,128)(2,1)S(1)} %copy-done, bf16[256,512]{1,0:T(8,128)(2,1)S(1)} %copy-done.1, f32[128,64]{1,0:T(8,128)S(1)} %copy-done.5, f32[128,64]{1,0:T(8,128)S(1)} %copy-done.4, f32[128,16]{1,0:T(8,128)S(1)} %copy-done.3, ...), custom_call_target="tpu_custom_call" | custom-call | tf_op jit(solution)/shard_map/spectra_gather/pallas_call | solution.py:199
  36.2 0.0 copy-start.6
  36.2 0.7 %copy-done.6 = f32[32,2,128]{2,1,0:T(2,128)S(1)} copy-done((f32[32,2,128]{2,1,0:T(2,128)S(1)}, f32[32,2,128]{2,1,0:T(2,128)}, u32[]{:S(2)}) %copy-start.6) | copy-done | bytes 32792
  36.9 8.6 %correlate.1 = f32[6,16,128,128]{3,2,1,0:T(8,128)} custom-call(s32[2]{0:T(128)S(1)} %pad_add_fusion.place, s32[6,1]{1,0:T(8,128)S(1)} %copy.12.partners, f32[32,2,128]{2,1,0:T(2,128)S(1)} %copy-done.6, bf16[128,1536]{1,0:T(8,128)(2,1)S(1)} %get-tuple-element.7.own_t, bf16[6,6,256,128]{3,2,1,0:T(8,128)(2,1)S(1)} %get-tuple-element.8.win), custom_call_target="tpu_custom_call" | custom-call | tf_op jit(solution)/shard_map/correlate/pallas_call | solution.py:227
Async XLA Ops:
  0.8 1.4 %copy-start = (bf16[3,2048,128]{2,1,0:T(8,128)(2,1)S(1)}, bf16[3,2048,128]{2,1,0:T(8,128)(2,1)}, u32[]{:S(2)}) copy-start(bf16[3,2048,128]{2,1,0:T(8,128)(2,1)} %rec.1) | copy-start | bytes 4718596
  2.2 0.9 %copy-start.1 = (bf16[256,512]{1,0:T(8,128)(2,1)S(1)}, bf16[256,512]{1,0:T(8,128)(2,1)}, u32[]{:S(2)}) copy-start(bf16[256,512]{1,0:T(8,128)(2,1)} %constant.20.clone.table) | copy-start | bytes 786436
  3.2 0.8 %copy-start.2 = (f32[128,16]{1,0:T(8,128)S(1)}, f32[128,16]{1,0:T(8,128)}, u32[]{:S(2)}) copy-start(f32[128,16]{1,0:T(8,128)} %constant.24.clone.white_sin) | copy-start | bytes 24580
  4.0 0.8 %copy-start.3 = (f32[128,16]{1,0:T(8,128)S(1)}, f32[128,16]{1,0:T(8,128)}, u32[]{:S(2)}) copy-start(f32[128,16]{1,0:T(8,128)} %constant.23.clone.white_cos) | copy-start | bytes 24580
  4.9 0.8 %copy-start.4 = (f32[128,64]{1,0:T(8,128)S(1)}, f32[128,64]{1,0:T(8,128)}, u32[]{:S(2)}) copy-start(f32[128,64]{1,0:T(8,128)} %constant.22.clone.band_sin) | copy-start | bytes 98308
  5.7 0.8 %copy-start.5 = (f32[128,64]{1,0:T(8,128)S(1)}, f32[128,64]{1,0:T(8,128)}, u32[]{:S(2)}) copy-start(f32[128,64]{1,0:T(8,128)} %constant.21.clone.band_cos) | copy-start | bytes 98308
  6.5 0.7 %copy-start.7 = (f32[16,128]{1,0:T(8,128)S(1)}, f32[16,128]{1,0:T(8,128)}, u32[]{:S(2)}) copy-start(f32[16,128]{1,0:T(8,128)} %white.1) | copy-start | bytes 24580
  7.2 0.7 %copy-start.8 = (f32[64]{0:T(128)S(1)}, f32[64]{0:T(128)}, u32[]{:S(2)}) copy-start(f32[64]{0:T(128)} %param.12) | copy-start | bytes 772
  7.9 0.7 %copy-start.9 = (s32[128]{0:T(128)S(1)}, s32[128]{0:T(128)}, u32[]{:S(2)}) copy-start(s32[128]{0:T(128)} %param.14) | copy-start | bytes 1540
  36.2 0.8 %copy-start.6 = (f32[32,2,128]{2,1,0:T(2,128)S(1)}, f32[32,2,128]{2,1,0:T(2,128)}, u32[]{:S(2)}) copy-start(f32[32,2,128]{2,1,0:T(2,128)} %constant.25.clone.lag_table) | copy-start | bytes 98308

commit v2 on v1

v2 whole, which is shorter than its diff:
```python
import functools
import math

import jax
import jax.numpy as jnp
import numpy as np
from jax import lax
from jax.experimental import pallas as pl
from jax.experimental.pallas import tpu as pltpu
from jax.sharding import PartitionSpec as P

NB = 128
SEG = 6
LAGS = 32
ROUNDS = 6
GROUP = 4
MESH = pl.DeviceIdType.MESH
VMEM = pltpu.VMEM
SMEM = pltpu.SMEM
ROLES = 6
WHOLE_VMEM = 63_480_000


def bin_numbers(samples):
    return samples // 64 + samples // (4 * NB) * np.arange(NB, dtype=np.int64)


def rotation(products, samples):
    angles = np.mod(products, samples) * (2.0 * math.pi / samples)
    return np.cos(angles), np.sin(angles)


def gather_kernel(
    count, segs,
    rec_in, table_in, band_table_in, white_table_in, lag_table_in, band_in, white_in, live_in,
    products,
    own, win, turned, staged, rec, table, band_table, white_table, lag_table, band, white, live,
    fetch, send, recv_x, recv_w, put,
):
    me = lax.axis_index("chan")
    tm = lax.axis_index("tm")
    core = lax.rem(me, 2)
    side = lax.rem(me // 2, 2)
    up = lax.rem(me + 4, count)
    down = lax.rem(me + count - 4, count)
    sib = me + 1 - 2 * core
    across = me + 2 - 4 * side
    other = 1 - tm
    lag_count, channels = lag_table.shape[0], own.shape[2]

    barrier = pltpu.get_barrier_semaphore()
    for peer in ((me, other), (up, tm), (down, tm), (across, tm), (sib, tm)):
        pl.semaphore_signal(barrier, inc=1, device_id=peer, device_id_type=MESH)

    pairs = [(band_in, band), (white_in, white), (live_in, live), (band_table_in, band_table),
             (white_table_in, white_table), (table_in, table)]
    pairs += [(rec_in.at[i], rec.at[i]) for i in range(segs)]
    pairs += [(lag_table_in.at[pl.ds(tm * lag_count, lag_count)], lag_table)]
    fetches = [pltpu.make_async_copy(src, dst, fetch.at[i]) for i, (src, dst) in enumerate(pairs)]
    for copy in fetches:
        copy.start()

    def seg_at(i):
        return tm * segs + i if i < segs else other * segs + (i - segs)

    sends = []

    def start(src, dst, sem, peer):
        copy = pltpu.make_async_remote_copy(
            src_ref=src, dst_ref=dst, send_sem=send.at[len(sends)], recv_sem=sem,
            device_id=peer, device_id_type=MESH,
        )
        copy.start()
        sends.append(copy)

    def arrived(dst, sem):
        pltpu.make_async_remote_copy(
            src_ref=dst, dst_ref=dst, send_sem=send.at[0], recv_sem=sem,
            device_id=(me, other), device_id_type=MESH,
        ).wait_recv()

    def wait_win(role, seg):
        arrived(win.at[role, seg], recv_w.at[role, seg])

    def spread(seg):
        for role, peer in ((2, up), (3, down), (1, across), (0, sib)):
            start(own.at[seg], win.at[role, seg], recv_w.at[role, seg], (peer, tm))

    mixed = lax.rem(core + side, 2)
    relay_src = 3 - side
    passing = segs + 5 * SEG

    def relay(i):
        seg = seg_at(i)
        wait_win(relay_src, seg)
        start(win.at[relay_src, seg], win.at[4, seg], recv_w.at[4, seg], (across, tm))

    def hand_on(role, i):
        seg = seg_at(i)
        wait_win(role, seg)

        @pl.when(mixed == role // 4)
        def _():
            pltpu.make_async_remote_copy(
                src_ref=win.at[role, seg], dst_ref=win.at[5, seg], send_sem=send.at[passing + i],
                recv_sem=recv_w.at[5, seg], device_id=(sib, tm), device_id_type=MESH,
            ).start()

    for copy in fetches[:5]:
        copy.wait()
    taps, band_count = band[...], band.shape[1]
    band_re = jnp.sum(band_table[:, :band_count] * taps, axis=1, keepdims=True)
    band_im = -jnp.sum(band_table[:, band_count:] * taps, axis=1, keepdims=True)
    white_resp = jnp.dot(
        white_table[...], white[...], precision=lax.Precision.HIGHEST, preferred_element_type=jnp.float32
    )
    white_re, white_im = white_resp[:NB], -white_resp[NB:]
    alive = live[...].astype(jnp.float32)
    resp_re = white_re * band_re - white_im * band_im
    resp_im = white_re * band_im + white_im * band_re

    period = table.shape[1]
    fetches[5].wait()
    for i in range(segs):
        fetches[6 + i].wait()
        raw = jnp.zeros((2 * NB, channels), jnp.float32)
        for first in range(0, rec.shape[1], period):
            raw = raw + jnp.dot(
                table[...], rec[i, first:first + period, :], preferred_element_type=jnp.float32
            )
        raw_re, raw_im = raw[:NB], raw[NB:]
        seg = seg_at(i)
        own[seg, :NB, :] = ((resp_re * raw_re - resp_im * raw_im) * alive).astype(jnp.bfloat16)
        own[seg, NB:, :] = ((resp_re * raw_im + resp_im * raw_re) * alive).astype(jnp.bfloat16)
        if i == 0:
            pl.semaphore_wait(barrier, 5)
        start(own.at[seg], own.at[seg], recv_x.at[i], (me, other))
        spread(seg)
    fetches[-1].wait()

    squares_own = jnp.zeros((channels, NB), jnp.float32)
    puts = []

    def turn(seg, total):
        re = own[seg, :NB, :].astype(jnp.float32).T
        im = own[seg, NB:, :].astype(jnp.float32).T
        at = pl.multiple_of(seg * 2 * NB, 2 * NB)

        def one_lag(l, carry):
            pair = lag_table[l]
            cos, sin = pair[0:1], pair[1:2]
            rows = pl.ds(pl.multiple_of(l * channels, channels), channels)
            turned[rows, pl.ds(at, NB)] = (re * cos - im * sin).astype(jnp.bfloat16)
            turned[rows, pl.ds(at + NB, NB)] = (re * sin + im * cos).astype(jnp.bfloat16)
            return carry

        lax.fori_loop(0, lag_count, one_lag, 0)
        return total + (re * re + im * im)

    def scales(roles, waited=None):
        squares = [jnp.zeros((8, channels), jnp.float32) for _ in roles]
        for i in range(2 * segs):
            seg = seg_at(i)
            if waited is not None:
                wait_win(waited, seg)
            for k, role in enumerate(roles):
                rows = win[role, seg].astype(jnp.float32)
                squares[k] += jnp.sum((rows * rows).reshape(-1, 8, channels), axis=0)
        means = [jnp.sum(part, axis=0, keepdims=True) / (SEG * NB) for part in squares]
        return jnp.concatenate([lax.rsqrt(mean + 1e-06) for mean in means], axis=1)

    def multiply(roles, scale, first, last):
        factor = own_scale * scale

        def one_group(g, carry):
            lags = pl.ds(g * GROUP, GROUP)
            rows = pl.ds(pl.multiple_of(g * GROUP * channels, GROUP * channels), GROUP * channels)
            chosen = jnp.concatenate([win[role].reshape(-1, channels) for role in roles], axis=1)
            sums = jnp.dot(turned[rows, :], chosen, preferred_element_type=jnp.float32)
            sums = sums.reshape(GROUP, channels, 2 * channels) * factor[None]
            for k, role in enumerate(roles):
                staged[role, lags] = sums[:, :, k * channels:(k + 1) * channels]
            return carry

        lax.fori_loop(first, last, one_group, 0)
        lags = pl.ds(first * GROUP, (last - first) * GROUP)
        for role in roles:
            copy = pltpu.make_async_copy(staged.at[role, lags], products.at[role, lags], put.at[len(puts)])
            copy.start()
            puts.append(copy)

    groups = lag_count // GROUP
    half = groups // 2
    for i in range(segs):
        seg = seg_at(segs + i)
        arrived(own.at[seg], recv_x.at[i])
        spread(seg)
        relay(i)
        hand_on(1, i)
        if i:
            hand_on(4, i - 1)
        squares_own = turn(seg_at(i), squares_own)
    relay(segs)
    hand_on(4, segs - 1)
    hand_on(1, segs)
    squares_own = turn(seg_at(segs), squares_own)
    squares_own = turn(seg_at(segs + 1), squares_own)
    relay(segs + 1)
    hand_on(4, segs)
    hand_on(1, segs + 1)
    hand_on(1, segs + 2)
    squares_own = turn(seg_at(segs + 2), squares_own)
    own_mean = jnp.sum(squares_own, axis=1, keepdims=True) / (SEG * NB)
    own_scale = lax.rsqrt(own_mean + 1e-06) * (1.0 / math.sqrt(SEG * NB))
    scale = scales((0, 1), 0)
    multiply((0, 1), scale, 0, groups)
    relay(segs + 2)
    hand_on(4, segs + 1)
    scale = scales((2, 3), 2 + side)
    multiply((2, 3), scale, 0, half)
    hand_on(4, segs + 2)
    multiply((2, 3), scale, half, groups)
    scale = scales((4, 5), 5)
    multiply((4, 5), scale, 0, half)
    multiply((4, 5), scale, half, groups)
    for copy in sends:
        copy.wait_send()
    for i in range(2 * segs):
        block = win.at[5, seg_at(i)]
        pltpu.make_async_remote_copy(
            src_ref=block, dst_ref=block, send_sem=send.at[passing + i], recv_sem=recv_w.at[5, seg_at(i)],
            device_id=(sib, tm), device_id_type=MESH,
        ).wait_send()
    for copy in puts:
        copy.wait()


def order_kernel(count, place, partners, products, out, sems):
    me = place[0]
    core = lax.rem(me, 2)
    side = lax.rem(me // 2, 2)
    offsets = (1 - 2 * core, 2 - 4 * side, -4, 4, 4 * side - 2, 2 * core - 1)
    copies = []
    for r in range(ROUNDS):
        delta = lax.rem(partners[r] - me + count + count // 2, count) - count // 2
        role = jnp.int32(0)
        for position, offset in enumerate(offsets):
            role = role + jnp.where(delta == offset, position, 0)
        for part in range(2):
            lags = pl.ds(part * (out.shape[1] // 2), out.shape[1] // 2)
            copies.append(pltpu.make_async_copy(products.at[role, lags], out.at[r, lags], sems.at[2 * r + part]))
            copies[-1].start()
    for copy in copies:
        copy.wait()


def local(records, band_taps, white_taps, live_mask, partners):
    segs, samples, channels = records.shape
    count = lax.axis_size("chan")
    inner = SEG * 2 * NB
    lag_count = LAGS // lax.axis_size("tm")
    bins = bin_numbers(samples)
    period = samples // math.gcd(samples, math.gcd(int(bins[0]), int(bins[1] - bins[0])))
    cos, sin = rotation(bins[:, None] * np.arange(period)[None, :], samples)
    table = np.concatenate([cos, -sin], axis=0).astype(np.float32).astype(jnp.bfloat16)
    band_table = np.concatenate(rotation(bins[:, None] * np.arange(band_taps.shape[0])[None, :], samples), axis=1)
    white_table = np.concatenate(rotation(bins[:, None] * np.arange(white_taps.shape[0])[None, :], samples), axis=0)
    lags = 3 * (np.arange(LAGS) - LAGS // 2)
    lag_table = np.stack(rotation(lags[:, None] * bins[None, :], samples), axis=1)
    f32 = lambda a: jnp.asarray(a.astype(np.float32))
    operands = (
        records, jnp.asarray(table), f32(band_table), f32(white_table), f32(lag_table),
        band_taps.reshape(1, -1), white_taps, live_mask.reshape(1, -1),
    )

    hbm = pl.BlockSpec(memory_space=pltpu.HBM)
    smem = pl.BlockSpec(memory_space=SMEM)
    shape = jax.ShapeDtypeStruct((ROLES, lag_count, channels, channels), jnp.float32)
    products = pl.pallas_call(
        functools.partial(gather_kernel, count, segs),
        out_shape=shape,
        in_specs=[hbm] * len(operands),
        out_specs=hbm,
        scratch_shapes=[
            VMEM((SEG, 2 * NB, channels), jnp.bfloat16),
            VMEM((ROLES, SEG, 2 * NB, channels), jnp.bfloat16),
            VMEM((lag_count * channels, inner), jnp.bfloat16),
            VMEM(shape.shape, jnp.float32),
            VMEM(records.shape, jnp.bfloat16),
            VMEM(table.shape, jnp.bfloat16),
            VMEM(band_table.shape, jnp.float32),
            VMEM(white_table.shape, jnp.float32),
            VMEM((lag_count, 2, NB), jnp.float32),
            VMEM((1, band_taps.shape[0]), jnp.float32),
            VMEM(white_taps.shape, jnp.float32),
            VMEM((1, channels), jnp.int32),
            pltpu.SemaphoreType.DMA((7 + segs,)),
            pltpu.SemaphoreType.DMA((segs + 6 * SEG,)),
            pltpu.SemaphoreType.DMA((segs,)),
            pltpu.SemaphoreType.DMA((ROLES, SEG)),
            pltpu.SemaphoreType.DMA((10,)),
        ],
        compiler_params=pltpu.CompilerParams(
            collective_id=0, has_side_effects=True, vmem_limit_bytes=WHOLE_VMEM
        ),
        name="spectra_gather",
    )(*operands)

    place = lax.axis_index("chan").astype(jnp.int32).reshape(1)
    return pl.pallas_call(
        functools.partial(order_kernel, count),
        out_shape=shape,
        in_specs=[smem, smem, hbm],
        out_specs=hbm,
        scratch_shapes=[pltpu.SemaphoreType.DMA((2 * ROUNDS,))],
        compiler_params=pltpu.CompilerParams(vmem_limit_bytes=WHOLE_VMEM),
        name="round_order",
    )(place, partners.reshape(-1), products)


def solution(mesh):
    return jax.shard_map(
        local,
        mesh=mesh,
        in_specs=(P("tm", None, "chan"), P(), P(None, "chan"), P("chan"), P(None, "chan")),
        out_specs=P(None, "tm", "chan", None),
        check_vma=False,
    )
```

time: 46 us -> 227 us (4.93)
  Pallas kernels: 36.2 us -> 227 us
  local copies, waits for them, and re-layouts: 9.21 us -> 0 us
    pallas_call x2, Pallas kernels: 36.2 us -> 227 us  [the longest x1 192 us: local(): pl.pallas_call(functools.partial(order_kernel, count), out_shape=shape, i...]
    unnamed x21 -> x0, local copies, waits for them, and re-layouts: 9.21 us -> none
where the time goes in v2:
time: 227 us
  Pallas kernels  227 us (100%)
    pallas_call x1, Pallas kernels, local(): pl.pallas_call(functools.partial(order_kernel, count), out_shape=shape, i...  192 us
    pallas_call x1, Pallas kernels, local(): pl.pallas_call(functools.partial(gather_kernel, count, segs), out_shape=s...  34.5 us

profile of v2, /device:TPU:0, one launch (start us, length us, event | category | flops | bytes accessed | tf_op | source)
XLA Modules:
  0.0 226.9 jit_solution(12609391881029682190)
XLA Ops:
  0.0 34.5 %spectra_gather.1.products = f32[6,16,128,128]{3,2,1,0:T(8,128)} custom-call(bf16[3,2048,128]{2,1,0:T(8,128)(2,1)} %rec_in.1, bf16[256,512]{1,0:T(8,128)(2,1)} %constant.14.clone.table_in, f32[128,128]{1,0:T(8,128)} %constant.15.clone.band_table_in, f32[256,16]{1,0:T(8,128)} %constant.16.clone.white_table_in, f32[32,2,128]{2,1,0:T(2,128)} %constant.17.clone.lag_table_in, ...), custom_call_target="tpu_custom_call" | custom-call | tf_op jit(solution)/shard_map/spectra_gather/pallas_call | solution.py:279
  34.5 192.5 %round_order.1 = f32[6,16,128,128]{3,2,1,0:T(8,128)} custom-call(s32[1]{0:T(128)} %bitcast.place, s32[6]{0:T(128)} %bitcast.6, f32[6,16,128,128]{3,2,1,0:T(8,128)} %spectra_gather.1.products), custom_call_target="tpu_custom_call" | custom-call | tf_op jit(solution)/shard_map/round_order/pallas_call | solution.py:310

commit v3 on v2

--- a/solution.py
+++ b/solution.py
@@ -13,7 +13,7 @@
 SEG = 6
 LAGS = 32
 ROUNDS = 6
-GROUP = 4
+GROUP = 8
 MESH = pl.DeviceIdType.MESH
 VMEM = pltpu.VMEM
 SMEM = pltpu.SMEM
@@ -65,13 +65,16 @@
 
     sends = []
 
-    def start(src, dst, sem, peer):
+    def start(src, dst, sem, peer, only=None):
         copy = pltpu.make_async_remote_copy(
             src_ref=src, dst_ref=dst, send_sem=send.at[len(sends)], recv_sem=sem,
             device_id=peer, device_id_type=MESH,
         )
-        copy.start()
-        sends.append(copy)
+        sends.append((copy, only))
+        if only is None:
+            copy.start()
+        else:
+            pl.when(only)(copy.start)
 
     def arrived(dst, sem):
         pltpu.make_async_remote_copy(
@@ -82,29 +85,37 @@
     def wait_win(role, seg):
         arrived(win.at[role, seg], recv_w.at[role, seg])
 
-    def spread(seg):
-        for role, peer in ((2, up), (3, down), (1, across), (0, sib)):
-            start(own.at[seg], win.at[role, seg], recv_w.at[role, seg], (peer, tm))
-
+    first_row, last_row = me < 4, me >= count - 4
     mixed = lax.rem(core + side, 2)
     relay_src = 3 - side
-    passing = segs + 5 * SEG
+    beyond = jnp.where(first_row, 2, 3)
+
+    def send_win(src, role, seg, peer, only=None):
+        start(src, win.at[role, seg], recv_w.at[role, seg], peer, only)
+
+    def spread(i):
+        seg = seg_at(i)
+        second = i >= segs
+        send_win(own.at[seg], 2, seg, (up, tm), jnp.logical_not(last_row) if second else None)
+        send_win(own.at[seg], 3, seg, (down, tm), jnp.logical_not(first_row) if second else None)
+        if not second:
+            send_win(own.at[seg], 1, seg, (across, tm))
+        send_win(own.at[seg], 0, seg, (sib, tm))
 
     def relay(i):
         seg = seg_at(i)
-        wait_win(relay_src, seg)
-        start(win.at[relay_src, seg], win.at[4, seg], recv_w.at[4, seg], (across, tm))
+        for role in (2, 3):
+            wait_win(role, seg)
+        send_win(win.at[relay_src, seg], 4, seg, (across, tm))
+        if i < segs:
+            send_win(win.at[beyond, seg], beyond, seg, (me, other), jnp.logical_or(first_row, last_row))
 
     def hand_on(role, i):
         seg = seg_at(i)
         wait_win(role, seg)
-
-        @pl.when(mixed == role // 4)
-        def _():
-            pltpu.make_async_remote_copy(
-                src_ref=win.at[role, seg], dst_ref=win.at[5, seg], send_sem=send.at[passing + i],
-                recv_sem=recv_w.at[5, seg], device_id=(sib, tm), device_id_type=MESH,
-            ).start()
+        if role == 1 and i < segs:
+            send_win(win.at[1, seg], 1, seg, (me, other))
+        send_win(win.at[role, seg], 5, seg, (sib, tm), mixed == role // 4)
 
     for copy in fetches[:5]:
         copy.wait()
@@ -135,7 +146,7 @@
         if i == 0:
             pl.semaphore_wait(barrier, 5)
         start(own.at[seg], own.at[seg], recv_x.at[i], (me, other))
-        spread(seg)
+        spread(i)
     fetches[-1].wait()
 
     squares_own = jnp.zeros((channels, NB), jnp.float32)
@@ -157,44 +168,47 @@
         lax.fori_loop(0, lag_count, one_lag, 0)
         return total + (re * re + im * im)
 
-    def scales(roles, waited=None):
-        squares = [jnp.zeros((8, channels), jnp.float32) for _ in roles]
-        for i in range(2 * segs):
+    def add_squares(totals, roles, places, waited=None):
+        totals = list(totals)
+        for i in places:
             seg = seg_at(i)
             if waited is not None:
                 wait_win(waited, seg)
             for k, role in enumerate(roles):
                 rows = win[role, seg].astype(jnp.float32)
-                squares[k] += jnp.sum((rows * rows).reshape(-1, 8, channels), axis=0)
-        means = [jnp.sum(part, axis=0, keepdims=True) / (SEG * NB) for part in squares]
-        return jnp.concatenate([lax.rsqrt(mean + 1e-06) for mean in means], axis=1)
-
-    def multiply(roles, scale, first, last):
-        factor = own_scale * scale
-
-        def one_group(g, carry):
+                totals[k] += jnp.sum((rows * rows).reshape(-1, 8, channels), axis=0)
+        return totals
+
+    def scales(totals):
+        means = [jnp.sum(part, axis=0, keepdims=True) / (SEG * NB) for part in totals]
+        return own_scale * jnp.concatenate([lax.rsqrt(mean + 1e-06) for mean in means], axis=1)
+
+    def multiply(roles, which, factor=None, groups=None):
+        span = pl.ds(which * segs, segs)
+        columns = pl.ds(pl.multiple_of(which * segs * 2 * NB, 2 * NB), segs * 2 * NB)
+        for g in groups or range(lag_count // GROUP):
             lags = pl.ds(g * GROUP, GROUP)
-            rows = pl.ds(pl.multiple_of(g * GROUP * channels, GROUP * channels), GROUP * channels)
-            chosen = jnp.concatenate([win[role].reshape(-1, channels) for role in roles], axis=1)
-            sums = jnp.dot(turned[rows, :], chosen, preferred_element_type=jnp.float32)
-            sums = sums.reshape(GROUP, channels, 2 * channels) * factor[None]
+            rows = pl.ds(g * GROUP * channels, GROUP * channels)
+            chosen = jnp.concatenate([win[role, span].reshape(-1, channels) for role in roles], axis=1)
+            sums = jnp.dot(turned[rows, columns], chosen, preferred_element_type=jnp.float32)
+            sums = sums.reshape(GROUP, channels, 2 * channels)
             for k, role in enumerate(roles):
-                staged[role, lags] = sums[:, :, k * channels:(k + 1) * channels]
-            return carry
-
-        lax.fori_loop(first, last, one_group, 0)
-        lags = pl.ds(first * GROUP, (last - first) * GROUP)
-        for role in roles:
-            copy = pltpu.make_async_copy(staged.at[role, lags], products.at[role, lags], put.at[len(puts)])
-            copy.start()
-            puts.append(copy)
-
-    groups = lag_count // GROUP
-    half = groups // 2
-    for i in range(segs):
-        seg = seg_at(segs + i)
-        arrived(own.at[seg], recv_x.at[i])
-        spread(seg)
+                mine = slice(k * channels, (k + 1) * channels)
+                if factor is None:
+                    staged[role, lags] = sums[:, :, mine]
+                else:
+                    staged[role, lags] = (staged[role, lags] + sums[:, :, mine]) * factor[:, mine][None]
+                    copy = pltpu.make_async_copy(
+                        staged.at[role, lags], products.at[role, lags], put.at[len(puts)]
+                    )
+                    copy.start()
+                    puts.append(copy)
+
+    firsts, seconds = range(segs), range(segs, 2 * segs)
+    nothing = [jnp.zeros((8, channels), jnp.float32)] * 2
+    for i in firsts:
+        arrived(own.at[seg_at(segs + i)], recv_x.at[i])
+        spread(segs + i)
         relay(i)
         hand_on(1, i)
         if i:
@@ -203,6 +217,8 @@
     relay(segs)
     hand_on(4, segs - 1)
     hand_on(1, segs)
+    multiply((2, 3), tm)
+    squares_b = add_squares(nothing, (2, 3), firsts)
     squares_own = turn(seg_at(segs), squares_own)
     squares_own = turn(seg_at(segs + 1), squares_own)
     relay(segs + 1)
@@ -212,46 +228,50 @@
     squares_own = turn(seg_at(segs + 2), squares_own)
     own_mean = jnp.sum(squares_own, axis=1, keepdims=True) / (SEG * NB)
     own_scale = lax.rsqrt(own_mean + 1e-06) * (1.0 / math.sqrt(SEG * NB))
-    scale = scales((0, 1), 0)
-    multiply((0, 1), scale, 0, groups)
+    squares_a = add_squares(nothing, (0, 1), range(2 * segs), 0)
+    multiply((0, 1), tm)
+    multiply((0, 1), other, scales(squares_a))
     relay(segs + 2)
     hand_on(4, segs + 1)
-    scale = scales((2, 3), 2 + side)
-    multiply((2, 3), scale, 0, half)
+    squares_c = add_squares(nothing, (4, 5), firsts, 5)
+    multiply((4, 5), tm)
     hand_on(4, segs + 2)
-    multiply((2, 3), scale, half, groups)
-    scale = scales((4, 5), 5)
-    multiply((4, 5), scale, 0, half)
-    multiply((4, 5), scale, half, groups)
-    for copy in sends:
-        copy.wait_send()
-    for i in range(2 * segs):
-        block = win.at[5, seg_at(i)]
-        pltpu.make_async_remote_copy(
-            src_ref=block, dst_ref=block, send_sem=send.at[passing + i], recv_sem=recv_w.at[5, seg_at(i)],
-            device_id=(sib, tm), device_id_type=MESH,
-        ).wait_send()
+    squares_b = add_squares(squares_b, (2, 3), seconds)
+    multiply((2, 3), other, scales(squares_b))
+    squares_c = add_squares(squares_c, (4, 5), seconds, 5)
+    multiply((4, 5), other, scales(squares_c))
+    for copy, only in sends:
+        if only is None:
+            copy.wait_send()
+        else:
+            pl.when(only)(copy.wait_send)
     for copy in puts:
         copy.wait()
 
 
-def order_kernel(count, place, partners, products, out, sems):
+def order_kernel(count, place, partners, products, out, held, get, put):
     me = place[0]
     core = lax.rem(me, 2)
     side = lax.rem(me // 2, 2)
     offsets = (1 - 2 * core, 2 - 4 * side, -4, 4, 4 * side - 2, 2 * core - 1)
-    copies = []
+    part = out.shape[1] // 2
+    gets, puts = [], []
     for r in range(ROUNDS):
         delta = lax.rem(partners[r] - me + count + count // 2, count) - count // 2
         role = jnp.int32(0)
         for position, offset in enumerate(offsets):
             role = role + jnp.where(delta == offset, position, 0)
-        for part in range(2):
-            lags = pl.ds(part * (out.shape[1] // 2), out.shape[1] // 2)
-            copies.append(pltpu.make_async_copy(products.at[role, lags], out.at[r, lags], sems.at[2 * r + part]))
-            copies[-1].start()
-    for copy in copies:
-        copy.wait()
+        for h in range(2):
+            k = 2 * r + h
+            lags = pl.ds(h * part, part)
+            gets.append(pltpu.make_async_copy(products.at[role, lags], held.at[r, lags], get.at[k]))
+            puts.append(pltpu.make_async_copy(held.at[r, lags], out.at[r, lags], put.at[k]))
+            gets[-1].start()
+    for into, onward in zip(gets, puts):
+        into.wait()
+        onward.start()
+    for onward in puts:
+        onward.wait()
 
 
 def local(records, band_taps, white_taps, live_mask, partners):
@@ -295,10 +315,10 @@
             VMEM(white_taps.shape, jnp.float32),
             VMEM((1, channels), jnp.int32),
             pltpu.SemaphoreType.DMA((7 + segs,)),
-            pltpu.SemaphoreType.DMA((segs + 6 * SEG,)),
+            pltpu.SemaphoreType.DMA((segs + 8 * SEG,)),
             pltpu.SemaphoreType.DMA((segs,)),
             pltpu.SemaphoreType.DMA((ROLES, SEG)),
-            pltpu.SemaphoreType.DMA((10,)),
+            pltpu.SemaphoreType.DMA((ROLES * lag_count // GROUP,)),
         ],
         compiler_params=pltpu.CompilerParams(
             collective_id=0, has_side_effects=True, vmem_limit_bytes=WHOLE_VMEM
@@ -312,7 +332,11 @@
         out_shape=shape,
         in_specs=[smem, smem, hbm],
         out_specs=hbm,
-        scratch_shapes=[pltpu.SemaphoreType.DMA((2 * ROUNDS,))],
+        scratch_shapes=[
+            VMEM(shape.shape, jnp.float32),
+            pltpu.SemaphoreType.DMA((2 * ROUNDS,)),
+            pltpu.SemaphoreType.DMA((2 * ROUNDS,)),
+        ],
         compiler_params=pltpu.CompilerParams(vmem_limit_bytes=WHOLE_VMEM),
         name="round_order",
     )(place, partners.reshape(-1), products)

time: 227 us -> 37.5 us (0.17)
  Pallas kernels: 227 us -> 37.3 us
    pallas_call x1, Pallas kernels: 192 us -> 6.16 us  [local(): pl.pallas_call(functools.partial(order_kernel, count), out_shape=shape, i...]
    pallas_call x1, Pallas kernels: 34.5 us -> 31.1 us  [local(): pl.pallas_call(functools.partial(gather_kernel, count, segs), out_shape=s...]
where the time goes in v3:
time: 37.5 us; the launch traced here: 37.3 us
  Pallas kernels  37.3 us (99%)
    pallas_call x1, Pallas kernels, local(): pl.pallas_call(functools.partial(gather_kernel, count, segs), out_shape=s...  31.1 us
    pallas_call x1, Pallas kernels, local(): pl.pallas_call(functools.partial(order_kernel, count), out_shape=shape, i...  6.16 us

profile of v3, /device:TPU:0, one launch (start us, length us, event | category | flops | bytes accessed | tf_op | source)
XLA Modules:
  0.0 37.3 jit_solution(8661710156899828655)
XLA Ops:
  0.0 31.1 %spectra_gather.1.products = f32[6,16,128,128]{3,2,1,0:T(8,128)} custom-call(bf16[3,2048,128]{2,1,0:T(8,128)(2,1)} %rec_in.1, bf16[256,512]{1,0:T(8,128)(2,1)} %constant.14.clone.table_in, f32[128,128]{1,0:T(8,128)} %constant.15.clone.band_table_in, f32[256,16]{1,0:T(8,128)} %constant.16.clone.white_table_in, f32[32,2,128]{2,1,0:T(2,128)} %constant.17.clone.lag_table_in, ...), custom_call_target="tpu_custom_call" | custom-call | tf_op jit(solution)/shard_map/spectra_gather/pallas_call | solution.py:299
  31.1 6.2 %round_order.1 = f32[6,16,128,128]{3,2,1,0:T(8,128)} custom-call(s32[1]{0:T(128)} %bitcast.place, s32[6]{0:T(128)} %bitcast.6, f32[6,16,128,128]{3,2,1,0:T(8,128)} %spectra_gather.1.products), custom_call_target="tpu_custom_call" | custom-call | tf_op jit(solution)/shard_map/round_order/pallas_call | solution.py:330

commit v4 on v3

--- a/solution.py
+++ b/solution.py
@@ -13,7 +13,7 @@
 SEG = 6
 LAGS = 32
 ROUNDS = 6
-GROUP = 8
+GROUP = 4
 MESH = pl.DeviceIdType.MESH
 VMEM = pltpu.VMEM
 SMEM = pltpu.SMEM
@@ -33,8 +33,8 @@
 def gather_kernel(
     count, segs,
     rec_in, table_in, band_table_in, white_table_in, lag_table_in, band_in, white_in, live_in,
-    products,
-    own, win, turned, staged, rec, table, band_table, white_table, lag_table, band, white, live,
+    win, turned_out, scale_out,
+    own, turned, own_scale, rec, table, band_table, white_table, lag_table, band, white, live,
     fetch, send, recv_x, recv_w, put,
 ):
     me = lax.axis_index("chan")
@@ -104,9 +104,9 @@
 
     def relay(i):
         seg = seg_at(i)
-        for role in (2, 3):
-            wait_win(role, seg)
+        wait_win(relay_src, seg)
         send_win(win.at[relay_src, seg], 4, seg, (across, tm))
+        wait_win(2 + side, seg)
         if i < segs:
             send_win(win.at[beyond, seg], beyond, seg, (me, other), jnp.logical_or(first_row, last_row))
 
@@ -152,94 +152,46 @@
     squares_own = jnp.zeros((channels, NB), jnp.float32)
     puts = []
 
-    def turn(seg, total):
+    def put_out(src, dst):
+        copy = pltpu.make_async_copy(src, dst, put.at[len(puts)])
+        copy.start()
+        puts.append(copy)
+
+    def turn(i, total):
+        seg = seg_at(i)
         re = own[seg, :NB, :].astype(jnp.float32).T
         im = own[seg, NB:, :].astype(jnp.float32).T
-        at = pl.multiple_of(seg * 2 * NB, 2 * NB)
 
         def one_lag(l, carry):
             pair = lag_table[l]
             cos, sin = pair[0:1], pair[1:2]
             rows = pl.ds(pl.multiple_of(l * channels, channels), channels)
-            turned[rows, pl.ds(at, NB)] = (re * cos - im * sin).astype(jnp.bfloat16)
-            turned[rows, pl.ds(at + NB, NB)] = (re * sin + im * cos).astype(jnp.bfloat16)
+            turned[seg, rows, :NB] = (re * cos - im * sin).astype(jnp.bfloat16)
+            turned[seg, rows, NB:] = (re * sin + im * cos).astype(jnp.bfloat16)
             return carry
 
         lax.fori_loop(0, lag_count, one_lag, 0)
+        put_out(turned.at[seg], turned_out.at[seg])
         return total + (re * re + im * im)
 
-    def add_squares(totals, roles, places, waited=None):
-        totals = list(totals)
-        for i in places:
-            seg = seg_at(i)
-            if waited is not None:
-                wait_win(waited, seg)
-            for k, role in enumerate(roles):
-                rows = win[role, seg].astype(jnp.float32)
-                totals[k] += jnp.sum((rows * rows).reshape(-1, 8, channels), axis=0)
-        return totals
-
-    def scales(totals):
-        means = [jnp.sum(part, axis=0, keepdims=True) / (SEG * NB) for part in totals]
-        return own_scale * jnp.concatenate([lax.rsqrt(mean + 1e-06) for mean in means], axis=1)
-
-    def multiply(roles, which, factor=None, groups=None):
-        span = pl.ds(which * segs, segs)
-        columns = pl.ds(pl.multiple_of(which * segs * 2 * NB, 2 * NB), segs * 2 * NB)
-        for g in groups or range(lag_count // GROUP):
-            lags = pl.ds(g * GROUP, GROUP)
-            rows = pl.ds(g * GROUP * channels, GROUP * channels)
-            chosen = jnp.concatenate([win[role, span].reshape(-1, channels) for role in roles], axis=1)
-            sums = jnp.dot(turned[rows, columns], chosen, preferred_element_type=jnp.float32)
-            sums = sums.reshape(GROUP, channels, 2 * channels)
-            for k, role in enumerate(roles):
-                mine = slice(k * channels, (k + 1) * channels)
-                if factor is None:
-                    staged[role, lags] = sums[:, :, mine]
-                else:
-                    staged[role, lags] = (staged[role, lags] + sums[:, :, mine]) * factor[:, mine][None]
-                    copy = pltpu.make_async_copy(
-                        staged.at[role, lags], products.at[role, lags], put.at[len(puts)]
-                    )
-                    copy.start()
-                    puts.append(copy)
-
-    firsts, seconds = range(segs), range(segs, 2 * segs)
-    nothing = [jnp.zeros((8, channels), jnp.float32)] * 2
-    for i in firsts:
-        arrived(own.at[seg_at(segs + i)], recv_x.at[i])
-        spread(segs + i)
+    for i in range(2 * segs):
+        if i < segs:
+            arrived(own.at[seg_at(segs + i)], recv_x.at[i])
+            spread(segs + i)
+        hand_on(1, i)
         relay(i)
-        hand_on(1, i)
         if i:
             hand_on(4, i - 1)
-        squares_own = turn(seg_at(i), squares_own)
-    relay(segs)
-    hand_on(4, segs - 1)
-    hand_on(1, segs)
-    multiply((2, 3), tm)
-    squares_b = add_squares(nothing, (2, 3), firsts)
-    squares_own = turn(seg_at(segs), squares_own)
-    squares_own = turn(seg_at(segs + 1), squares_own)
-    relay(segs + 1)
-    hand_on(4, segs)
-    hand_on(1, segs + 1)
-    hand_on(1, segs + 2)
-    squares_own = turn(seg_at(segs + 2), squares_own)
+        squares_own = turn(i, squares_own)
     own_mean = jnp.sum(squares_own, axis=1, keepdims=True) / (SEG * NB)
-    own_scale = lax.rsqrt(own_mean + 1e-06) * (1.0 / math.sqrt(SEG * NB))
-    squares_a = add_squares(nothing, (0, 1), range(2 * segs), 0)
-    multiply((0, 1), tm)
-    multiply((0, 1), other, scales(squares_a))
-    relay(segs + 2)
-    hand_on(4, segs + 1)
-    squares_c = add_squares(nothing, (4, 5), firsts, 5)
-    multiply((4, 5), tm)
-    hand_on(4, segs + 2)
-    squares_b = add_squares(squares_b, (2, 3), seconds)
-    multiply((2, 3), other, scales(squares_b))
-    squares_c = add_squares(squares_c, (4, 5), seconds, 5)
-    multiply((4, 5), other, scales(squares_c))
+    own_scale[...] = jnp.broadcast_to(
+        lax.rsqrt(own_mean + 1e-06) * (1.0 / math.sqrt(SEG * NB)), own_scale.shape
+    )
+    put_out(own_scale, scale_out)
+    hand_on(4, 2 * segs - 1)
+    for role in (0, 5):
+        for i in range(2 * segs):
+            wait_win(role, seg_at(i))
     for copy, only in sends:
         if only is None:
             copy.wait_send()
@@ -249,35 +201,43 @@
         copy.wait()
 
 
-def order_kernel(count, place, partners, products, out, held, get, put):
+def correlate_kernel(count, place, partners, turned, win, own_scale, out, factor):
     me = place[0]
     core = lax.rem(me, 2)
     side = lax.rem(me // 2, 2)
     offsets = (1 - 2 * core, 2 - 4 * side, -4, 4, 4 * side - 2, 2 * core - 1)
-    part = out.shape[1] // 2
-    gets, puts = [], []
-    for r in range(ROUNDS):
+    channels = win.shape[3]
+
+    @pl.when(pl.program_id(0) == 0)
+    def _():
+        for role in range(ROLES):
+            total = jnp.zeros((8, channels), jnp.float32)
+            for seg in range(SEG):
+                rows = win[role, seg].astype(jnp.float32)
+                total += jnp.sum((rows * rows).reshape(-1, 8, channels), axis=0)
+            mean = jnp.sum(total, axis=0, keepdims=True) / (SEG * NB)
+            factor[role] = own_scale[...] * lax.rsqrt(mean + 1e-06)
+
+    def role_of(r):
         delta = lax.rem(partners[r] - me + count + count // 2, count) - count // 2
         role = jnp.int32(0)
         for position, offset in enumerate(offsets):
             role = role + jnp.where(delta == offset, position, 0)
-        for h in range(2):
-            k = 2 * r + h
-            lags = pl.ds(h * part, part)
-            gets.append(pltpu.make_async_copy(products.at[role, lags], held.at[r, lags], get.at[k]))
-            puts.append(pltpu.make_async_copy(held.at[r, lags], out.at[r, lags], put.at[k]))
-            gets[-1].start()
-    for into, onward in zip(gets, puts):
-        into.wait()
-        onward.start()
-    for onward in puts:
-        onward.wait()
+        return role
+
+    left = jnp.concatenate([turned[seg] for seg in range(SEG)], axis=1)
+    for r in range(0, ROUNDS, 2):
+        roles = (role_of(r), role_of(r + 1))
+        chosen = jnp.concatenate([win[role].reshape(-1, channels) for role in roles], axis=1)
+        sums = jnp.dot(left, chosen, preferred_element_type=jnp.float32)
+        for k in range(2):
+            part = sums[:, k * channels:(k + 1) * channels].reshape(GROUP, channels, channels)
+            out[r + k] = part * factor[roles[k]][None]
 
 
 def local(records, band_taps, white_taps, live_mask, partners):
     segs, samples, channels = records.shape
     count = lax.axis_size("chan")
-    inner = SEG * 2 * NB
     lag_count = LAGS // lax.axis_size("tm")
     bins = bin_numbers(samples)
     period = samples // math.gcd(samples, math.gcd(int(bins[0]), int(bins[1] - bins[0])))
@@ -295,17 +255,19 @@
 
     hbm = pl.BlockSpec(memory_space=pltpu.HBM)
     smem = pl.BlockSpec(memory_space=SMEM)
-    shape = jax.ShapeDtypeStruct((ROLES, lag_count, channels, channels), jnp.float32)
-    products = pl.pallas_call(
+    win, turned, own_scale = pl.pallas_call(
         functools.partial(gather_kernel, count, segs),
-        out_shape=shape,
+        out_shape=(
+            jax.ShapeDtypeStruct((ROLES, SEG, 2 * NB, channels), jnp.bfloat16),
+            jax.ShapeDtypeStruct((SEG, lag_count * channels, 2 * NB), jnp.bfloat16),
+            jax.ShapeDtypeStruct((channels, channels), jnp.float32),
+        ),
         in_specs=[hbm] * len(operands),
-        out_specs=hbm,
+        out_specs=(hbm, hbm, hbm),
         scratch_shapes=[
             VMEM((SEG, 2 * NB, channels), jnp.bfloat16),
-            VMEM((ROLES, SEG, 2 * NB, channels), jnp.bfloat16),
-            VMEM((lag_count * channels, inner), jnp.bfloat16),
-            VMEM(shape.shape, jnp.float32),
+            VMEM((SEG, lag_count * channels, 2 * NB), jnp.bfloat16),
+            VMEM((channels, channels), jnp.float32),
             VMEM(records.shape, jnp.bfloat16),
             VMEM(table.shape, jnp.bfloat16),
             VMEM(band_table.shape, jnp.float32),
@@ -318,7 +280,7 @@
             pltpu.SemaphoreType.DMA((segs + 8 * SEG,)),
             pltpu.SemaphoreType.DMA((segs,)),
             pltpu.SemaphoreType.DMA((ROLES, SEG)),
-            pltpu.SemaphoreType.DMA((ROLES * lag_count // GROUP,)),
+            pltpu.SemaphoreType.DMA((SEG + 1,)),
         ],
         compiler_params=pltpu.CompilerParams(
             collective_id=0, has_side_effects=True, vmem_limit_bytes=WHOLE_VMEM
@@ -328,18 +290,20 @@
 
     place = lax.axis_index("chan").astype(jnp.int32).reshape(1)
     return pl.pallas_call(
-        functools.partial(order_kernel, count),
-        out_shape=shape,
-        in_specs=[smem, smem, hbm],
-        out_specs=hbm,
-        scratch_shapes=[
-            VMEM(shape.shape, jnp.float32),
-            pltpu.SemaphoreType.DMA((2 * ROUNDS,)),
-            pltpu.SemaphoreType.DMA((2 * ROUNDS,)),
+        functools.partial(correlate_kernel, count),
+        grid=(lag_count // GROUP,),
+        out_shape=jax.ShapeDtypeStruct((ROUNDS, lag_count, channels, channels), jnp.float32),
+        in_specs=[
+            smem, smem,
+            pl.BlockSpec((SEG, GROUP * channels, 2 * NB), lambda i: (0, i, 0)),
+            pl.BlockSpec(win.shape, lambda i: (0, 0, 0, 0)),
+            pl.BlockSpec(own_scale.shape, lambda i: (0, 0)),
         ],
+        out_specs=pl.BlockSpec((ROUNDS, GROUP, channels, channels), lambda i: (0, i, 0, 0)),
+        scratch_shapes=[VMEM((ROLES, channels, channels), jnp.float32)],
         compiler_params=pltpu.CompilerParams(vmem_limit_bytes=WHOLE_VMEM),
-        name="round_order",
-    )(place, partners.reshape(-1), products)
+        name="correlate",
+    )(place, partners.reshape(-1), turned, win, own_scale)
 
 
 def solution(mesh):

time: 37.5 us -> 37.5 us (level)
  no operation moved by 1% of the time
where the time goes in v4:
time: 37.5 us; the launch traced here: 37.3 us
  Pallas kernels  37.3 us (99%)
    pallas_call x1, Pallas kernels, local(): pl.pallas_call(functools.partial(gather_kernel, count, segs), out_shape=(...  27.1 us
    pallas_call x1, Pallas kernels, local(): pl.pallas_call(functools.partial(correlate_kernel, count), grid=(lag_coun...  10.3 us

profile of v4, /device:TPU:0, one launch (start us, length us, event | category | flops | bytes accessed | tf_op | source)
XLA Modules:
  0.0 37.3 jit_solution(12723692828384137751)
XLA Ops:
  0.0 27.1 %spectra_gather.1 = (bf16[6,6,256,128]{3,2,1,0:T(8,128)(2,1)}, bf16[6,2048,256]{2,1,0:T(8,128)(2,1)}, f32[128,128]{1,0:T(8,128)}) custom-call(bf16[3,2048,128]{2,1,0:T(8,128)(2,1)} %rec_in.1, bf16[256,512]{1,0:T(8,128)(2,1)} %constant.14.clone.table_in, f32[128,128]{1,0:T(8,128)} %constant.15.clone.band_table_in, f32[256,16]{1,0:T(8,128)} %constant.16.clone.white_table_in, ...), custom_call_target="tpu_custom_call" | custom-call | tf_op jit(solution)/shard_map/spectra_gather/pallas_call | solution.py:258
  27.1 10.3 %correlate.1 = f32[6,16,128,128]{3,2,1,0:T(8,128)} custom-call(s32[1]{0:T(128)} %bitcast.place, s32[6]{0:T(128)} %bitcast.6, bf16[6,2048,256]{2,1,0:T(8,128)(2,1)} %get-tuple-element.8.turned, bf16[6,6,256,128]{3,2,1,0:T(8,128)(2,1)} %get-tuple-element.9.win, f32[128,128]{1,0:T(8,128)} %get-tuple-element.10.own_scale), custom_call_target="tpu_custom_call" | custom-call | tf_op jit(solution)/shard_map/correlate/pallas_call | solution.py:292

commit v5 on v4

v5 whole, which is shorter than its diff:
```python
import functools
import math

import jax
import jax.numpy as jnp
import numpy as np
from jax import lax
from jax.experimental import pallas as pl
from jax.experimental.pallas import tpu as pltpu
from jax.sharding import PartitionSpec as P

NB = 128
SEG = 6
LAGS = 32
ROUNDS = 6
GROUP = 8
MESH = pl.DeviceIdType.MESH
VMEM = pltpu.VMEM
SMEM = pltpu.SMEM
ROLES = 6
WHOLE_VMEM = 63_480_000


def bin_numbers(samples):
    return samples // 64 + samples // (4 * NB) * np.arange(NB, dtype=np.int64)


def rotation(products, samples):
    angles = np.mod(products, samples) * (2.0 * math.pi / samples)
    return np.cos(angles), np.sin(angles)


def gather_kernel(
    count, segs,
    rec_in, table_in, band_table_in, white_table_in, lag_table_in, band_in, white_in, live_in,
    partners, out,
    own, win_a, win_b, turned_a, turned_b, staged, win_scale, rec, table, band_table, white_table, lag_table, band, white, live,
    fetch, send, recv_x, recv_w, put,
):
    me = lax.axis_index("chan")
    tm = lax.axis_index("tm")
    core = lax.rem(me, 2)
    side = lax.rem(me // 2, 2)
    up = lax.rem(me + 4, count)
    down = lax.rem(me + count - 4, count)
    sib = me + 1 - 2 * core
    across = me + 2 - 4 * side
    other = 1 - tm
    lag_count, channels = lag_table.shape[0], own.shape[2]

    barrier = pltpu.get_barrier_semaphore()
    for peer in ((me, other), (up, tm), (down, tm), (across, tm), (sib, tm)):
        pl.semaphore_signal(barrier, inc=1, device_id=peer, device_id_type=MESH)

    pairs = [(band_in, band), (white_in, white), (live_in, live), (band_table_in, band_table),
             (white_table_in, white_table), (table_in, table)]
    pairs += [(rec_in.at[i], rec.at[i]) for i in range(segs)]
    pairs += [(lag_table_in.at[pl.ds(tm * lag_count, lag_count)], lag_table)]
    fetches = [pltpu.make_async_copy(src, dst, fetch.at[i]) for i, (src, dst) in enumerate(pairs)]
    for copy in fetches:
        copy.start()

    def win_at(role, i):
        return win_a.at[role, i] if i < segs else win_b.at[role, i - segs]

    sends = []

    def start(src, dst, sem, peer, only=None):
        copy = pltpu.make_async_remote_copy(
            src_ref=src, dst_ref=dst, send_sem=send.at[len(sends)], recv_sem=sem,
            device_id=peer, device_id_type=MESH,
        )
        sends.append((copy, only))
        if only is None:
            copy.start()
        else:
            pl.when(only)(copy.start)

    def arrived(dst, sem):
        pltpu.make_async_remote_copy(
            src_ref=dst, dst_ref=dst, send_sem=send.at[0], recv_sem=sem,
            device_id=(me, other), device_id_type=MESH,
        ).wait_recv()

    def wait_win(role, i):
        arrived(win_at(role, i), recv_w.at[role, i])

    first_row, last_row = me < 4, me >= count - 4
    mixed = lax.rem(core + side, 2)
    relay_src = 3 - side
    beyond = jnp.where(first_row, 2, 3)

    def send_win(src, role, i, peer, only=None):
        start(src, win_at(role, i), recv_w.at[role, i], peer, only)

    def spread(i):
        second = i >= segs
        send_win(own.at[i], 2, i, (up, tm), jnp.logical_not(last_row) if second else None)
        send_win(own.at[i], 3, i, (down, tm), jnp.logical_not(first_row) if second else None)
        if not second:
            send_win(own.at[i], 1, i, (across, tm))
        send_win(own.at[i], 0, i, (sib, tm))

    def relay(i):
        wait_win(relay_src, i)
        send_win(win_at(relay_src, i), 4, i, (across, tm))
        wait_win(2 + side, i)
        if i < segs:
            send_win(win_at(beyond, i), beyond, segs + i, (me, other), jnp.logical_or(first_row, last_row))

    def hand_on(role, i):
        wait_win(role, i)
        if role == 1 and i < segs:
            send_win(win_at(1, i), 1, segs + i, (me, other))
        send_win(win_at(role, i), 5, i, (sib, tm), mixed == role // 4)

    for copy in fetches[:5]:
        copy.wait()
    taps, band_count = band[...], band.shape[1]
    band_re = jnp.sum(band_table[:, :band_count] * taps, axis=1, keepdims=True)
    band_im = -jnp.sum(band_table[:, band_count:] * taps, axis=1, keepdims=True)
    white_resp = jnp.dot(
        white_table[...], white[...], precision=lax.Precision.HIGHEST, preferred_element_type=jnp.float32
    )
    white_re, white_im = white_resp[:NB], -white_resp[NB:]
    alive = live[...].astype(jnp.float32)
    resp_re = white_re * band_re - white_im * band_im
    resp_im = white_re * band_im + white_im * band_re

    period = table.shape[1]
    fetches[5].wait()
    for i in range(segs):
        fetches[6 + i].wait()
        raw = jnp.zeros((2 * NB, channels), jnp.float32)
        for first in range(0, rec.shape[1], period):
            raw = raw + jnp.dot(
                table[...], rec[i, first:first + period, :], preferred_element_type=jnp.float32
            )
        raw_re, raw_im = raw[:NB], raw[NB:]
        own[i, :NB, :] = ((resp_re * raw_re - resp_im * raw_im) * alive).astype(jnp.bfloat16)
        own[i, NB:, :] = ((resp_re * raw_im + resp_im * raw_re) * alive).astype(jnp.bfloat16)
        if i == 0:
            pl.semaphore_wait(barrier, 5)
        start(own.at[i], own.at[segs + i], recv_x.at[i], (me, other))
        spread(i)
    fetches[-1].wait()

    squares_own = jnp.zeros((channels, NB), jnp.float32)
    puts = []

    def turn(i, total):
        re = own[i, :NB, :].astype(jnp.float32).T
        im = own[i, NB:, :].astype(jnp.float32).T
        turned = turned_a if i < segs else turned_b
        at = (i % segs) * 2 * NB

        def one_lag(l, carry):
            pair = lag_table[l]
            cos, sin = pair[0:1], pair[1:2]
            rows = pl.ds(pl.multiple_of(l * channels, channels), channels)
            turned[rows, at:at + NB] = (re * cos - im * sin).astype(jnp.bfloat16)
            turned[rows, at + NB:at + 2 * NB] = (re * sin + im * cos).astype(jnp.bfloat16)
            return carry

        lax.fori_loop(0, lag_count, one_lag, 0)
        return total + (re * re + im * im)

    def add_squares(totals, win):
        totals = list(totals)
        for role in range(ROLES):
            for i in range(segs):
                rows = win[role, i].astype(jnp.float32)
                totals[role] += jnp.sum((rows * rows).reshape(-1, 8, channels), axis=0)
        return totals

    offsets = (1 - 2 * core, 2 - 4 * side, -4, 4, 4 * side - 2, 2 * core - 1)
    roles = []
    for r in range(ROUNDS):
        delta = lax.rem(partners[r] - me + count + count // 2, count) - count // 2
        role = jnp.int32(0)
        for position, offset in enumerate(offsets):
            role = role + jnp.where(delta == offset, position, 0)
        roles.append(role)

    def multiply(r, turned, win, factor=None):
        for g in range(lag_count // GROUP):
            lags = pl.ds(g * GROUP, GROUP)
            rows = pl.ds(g * GROUP * channels, GROUP * channels)
            chosen = jnp.concatenate([win[roles[r + k]].reshape(-1, channels) for k in range(2)], axis=1)
            sums = jnp.dot(turned[rows, :], chosen, preferred_element_type=jnp.float32)
            sums = sums.reshape(GROUP, channels, 2 * channels)
            for k in range(2):
                mine = slice(k * channels, (k + 1) * channels)
                if factor is None:
                    staged[r + k, lags] = sums[:, :, mine]
                else:
                    staged[r + k, lags] = (staged[r + k, lags] + sums[:, :, mine]) * factor[k][None]
                    copy = pltpu.make_async_copy(
                        staged.at[r + k, lags], out.at[r + k, lags], put.at[len(puts)]
                    )
                    copy.start()
                    puts.append(copy)

    squares_win = [jnp.zeros((8, channels), jnp.float32)] * ROLES
    for i in range(segs):
        arrived(own.at[segs + i], recv_x.at[i])
        spread(segs + i)
        hand_on(1, i)
        relay(i)
        if i:
            hand_on(4, i - 1)
        squares_own = turn(i, squares_own)
    for i in range(segs, 2 * segs):
        hand_on(1, i)
        relay(i)
        hand_on(4, i - 1)
        if i == segs:
            squares_own = turn(segs, squares_own)
            squares_own = turn(segs + 1, squares_own)
        if i == segs + 1:
            squares_own = turn(segs + 2, squares_own)
            for role in (0, 5):
                for j in range(segs):
                    wait_win(role, j)
            multiply(0, turned_a, win_a)
    multiply(2, turned_a, win_a)
    squares_win = add_squares(squares_win, win_a)
    hand_on(4, 2 * segs - 1)
    multiply(4, turned_a, win_a)
    own_mean = jnp.sum(squares_own, axis=1, keepdims=True) / (SEG * NB)
    own_scale = lax.rsqrt(own_mean + 1e-06) * (1.0 / math.sqrt(SEG * NB))
    for role in (0, 5):
        for i in range(segs, 2 * segs):
            wait_win(role, i)
    squares_win = add_squares(squares_win, win_b)
    for role in range(ROLES):
        mean = jnp.sum(squares_win[role], axis=0, keepdims=True) / (SEG * NB)
        win_scale[role] = lax.rsqrt(mean + 1e-06)
    for r in range(0, ROUNDS, 2):
        factor = [own_scale * win_scale[roles[r + k]] for k in range(2)]
        multiply(r, turned_b, win_b, factor)
    for copy, only in sends:
        if only is None:
            copy.wait_send()
        else:
            pl.when(only)(copy.wait_send)
    for copy in puts:
        copy.wait()


def local(records, band_taps, white_taps, live_mask, partners):
    segs, samples, channels = records.shape
    count = lax.axis_size("chan")
    lag_count = LAGS // lax.axis_size("tm")
    bins = bin_numbers(samples)
    period = samples // math.gcd(samples, math.gcd(int(bins[0]), int(bins[1] - bins[0])))
    cos, sin = rotation(bins[:, None] * np.arange(period)[None, :], samples)
    table = np.concatenate([cos, -sin], axis=0).astype(np.float32).astype(jnp.bfloat16)
    band_table = np.concatenate(rotation(bins[:, None] * np.arange(band_taps.shape[0])[None, :], samples), axis=1)
    white_table = np.concatenate(rotation(bins[:, None] * np.arange(white_taps.shape[0])[None, :], samples), axis=0)
    lags = 3 * (np.arange(LAGS) - LAGS // 2)
    lag_table = np.stack(rotation(lags[:, None] * bins[None, :], samples), axis=1)
    f32 = lambda a: jnp.asarray(a.astype(np.float32))
    operands = (
        records, jnp.asarray(table), f32(band_table), f32(white_table), f32(lag_table),
        band_taps.reshape(1, -1), white_taps, live_mask.reshape(1, -1),
    )

    hbm = pl.BlockSpec(memory_space=pltpu.HBM)
    smem = pl.BlockSpec(memory_space=SMEM)
    half = segs * 2 * NB
    shape = (ROUNDS, lag_count, channels, channels)
    return pl.pallas_call(
        functools.partial(gather_kernel, count, segs),
        out_shape=jax.ShapeDtypeStruct(shape, jnp.float32),
        in_specs=[hbm] * len(operands) + [smem],
        out_specs=hbm,
        scratch_shapes=[
            VMEM((SEG, 2 * NB, channels), jnp.bfloat16),
            VMEM((ROLES, segs, 2 * NB, channels), jnp.bfloat16),
            VMEM((ROLES, segs, 2 * NB, channels), jnp.bfloat16),
            VMEM((lag_count * channels, half), jnp.bfloat16),
            VMEM((lag_count * channels, half), jnp.bfloat16),
            VMEM(shape, jnp.float32),
            VMEM((ROLES, 1, channels), jnp.float32),
            VMEM(records.shape, jnp.bfloat16),
            VMEM(table.shape, jnp.bfloat16),
            VMEM(band_table.shape, jnp.float32),
            VMEM(white_table.shape, jnp.float32),
            VMEM((lag_count, 2, NB), jnp.float32),
            VMEM((1, band_taps.shape[0]), jnp.float32),
            VMEM(white_taps.shape, jnp.float32),
            VMEM((1, channels), jnp.int32),
            pltpu.SemaphoreType.DMA((7 + segs,)),
            pltpu.SemaphoreType.DMA((segs + 8 * SEG,)),
            pltpu.SemaphoreType.DMA((segs,)),
            pltpu.SemaphoreType.DMA((ROLES, SEG)),
            pltpu.SemaphoreType.DMA((ROUNDS * lag_count // GROUP,)),
        ],
        compiler_params=pltpu.CompilerParams(
            collective_id=0, has_side_effects=True, vmem_limit_bytes=WHOLE_VMEM
        ),
        name="correlations",
    )(*operands, partners.reshape(-1))


def solution(mesh):
    return jax.shard_map(
        local,
        mesh=mesh,
        in_specs=(P("tm", None, "chan"), P(), P(None, "chan"), P("chan"), P(None, "chan")),
        out_specs=P(None, "tm", "chan", None),
        check_vma=False,
    )
```

time: 37.5 us -> 39.4 us (1.051)
  local copies, waits for them, and re-layouts: 0 us -> 6.29 us
  Pallas kernels: 37.3 us -> 32.9 us
    unnamed x0 -> x1, local copies, waits for them, and re-layouts: none -> 6.29 us
    pallas_call x2 -> x1, Pallas kernels: 37.3 us -> 32.9 us  [local(): pl.pallas_call(functools.partial(gather_kernel, count, segs), out_shape=j...]
where the time goes in v5:
time: 39.4 us; the launch traced here: 39.2 us
  Pallas kernels  32.9 us (84%)
  local copies, waits for them, and re-layouts  6.29 us (16%)
    pallas_call x1, Pallas kernels, local(): pl.pallas_call(functools.partial(gather_kernel, count, segs), out_shape=j...  32.9 us
    unnamed x1, local copies, waits for them, and re-layouts  6.29 us

profile of v5, /device:TPU:0, one launch (start us, length us, event | category | flops | bytes accessed | tf_op | source)
XLA Modules:
  0.0 39.2 jit_solution(3231473748699335154)
XLA Ops:
  0.0 32.9 %correlations.1 = f32[6,16,128,128]{3,2,1,0:T(8,128)} custom-call(bf16[3,2048,128]{2,1,0:T(8,128)(2,1)} %rec_in.1, bf16[256,512]{1,0:T(8,128)(2,1)} %constant.8.clone.table_in, f32[128,128]{1,0:T(8,128)} %constant.9.clone.band_table_in, f32[256,16]{1,0:T(8,128)} %constant.10.clone.white_table_in, f32[32,2,128]{2,1,0:T(2,128)} %constant.11.clone.lag_table_in, ...), custom_call_target="tpu_custom_call" | custom-call | tf_op jit(solution)/shard_map/correlations/pallas_call | solution.py:273
  32.9 6.3 %copy.11 = f32[6,16,128,128]{3,2,1,0:T(8,128)} copy(f32[6,16,128,128]{3,2,1,0:T(8,128)} %correlations.1) | data formatting | bytes 12582912

commit v6 on v4

--- a/solution.py
+++ b/solution.py
@@ -32,9 +32,9 @@
 
 def gather_kernel(
     count, segs,
-    rec_in, table_in, band_table_in, white_table_in, lag_table_in, band_in, white_in, live_in,
-    win, turned_out, scale_out,
-    own, turned, own_scale, rec, table, band_table, white_table, lag_table, band, white, live,
+    rec_in, table_in, band_table_in, white_table_in, band_in, white_in, live_in,
+    win, own_out,
+    own, own_t, rec, table, band_table, white_table, band, white, live,
     fetch, send, recv_x, recv_w, put,
 ):
     me = lax.axis_index("chan")
@@ -46,7 +46,7 @@
     sib = me + 1 - 2 * core
     across = me + 2 - 4 * side
     other = 1 - tm
-    lag_count, channels = lag_table.shape[0], own.shape[2]
+    channels = own.shape[2]
 
     barrier = pltpu.get_barrier_semaphore()
     for peer in ((me, other), (up, tm), (down, tm), (across, tm), (sib, tm)):
@@ -55,7 +55,6 @@
     pairs = [(band_in, band), (white_in, white), (live_in, live), (band_table_in, band_table),
              (white_table_in, white_table), (table_in, table)]
     pairs += [(rec_in.at[i], rec.at[i]) for i in range(segs)]
-    pairs += [(lag_table_in.at[pl.ds(tm * lag_count, lag_count)], lag_table)]
     fetches = [pltpu.make_async_copy(src, dst, fetch.at[i]) for i, (src, dst) in enumerate(pairs)]
     for copy in fetches:
         copy.start()
@@ -147,32 +146,11 @@
             pl.semaphore_wait(barrier, 5)
         start(own.at[seg], own.at[seg], recv_x.at[i], (me, other))
         spread(i)
-    fetches[-1].wait()
-
-    squares_own = jnp.zeros((channels, NB), jnp.float32)
-    puts = []
-
-    def put_out(src, dst):
-        copy = pltpu.make_async_copy(src, dst, put.at[len(puts)])
-        copy.start()
-        puts.append(copy)
-
-    def turn(i, total):
-        seg = seg_at(i)
-        re = own[seg, :NB, :].astype(jnp.float32).T
-        im = own[seg, NB:, :].astype(jnp.float32).T
-
-        def one_lag(l, carry):
-            pair = lag_table[l]
-            cos, sin = pair[0:1], pair[1:2]
-            rows = pl.ds(pl.multiple_of(l * channels, channels), channels)
-            turned[seg, rows, :NB] = (re * cos - im * sin).astype(jnp.bfloat16)
-            turned[seg, rows, NB:] = (re * sin + im * cos).astype(jnp.bfloat16)
-            return carry
-
-        lax.fori_loop(0, lag_count, one_lag, 0)
-        put_out(turned.at[seg], turned_out.at[seg])
-        return total + (re * re + im * im)
+
+    def transpose(i):
+        seg = seg_at(i)
+        for part in (slice(0, NB), slice(NB, 2 * NB)):
+            own_t[seg, :, part] = own[seg, part, :].astype(jnp.float32).T.astype(jnp.bfloat16)
 
     for i in range(2 * segs):
         if i < segs:
@@ -182,12 +160,11 @@
         relay(i)
         if i:
             hand_on(4, i - 1)
-        squares_own = turn(i, squares_own)
-    own_mean = jnp.sum(squares_own, axis=1, keepdims=True) / (SEG * NB)
-    own_scale[...] = jnp.broadcast_to(
-        lax.rsqrt(own_mean + 1e-06) * (1.0 / math.sqrt(SEG * NB)), own_scale.shape
-    )
-    put_out(own_scale, scale_out)
+        if i >= segs:
+            transpose(i - segs)
+            transpose(i)
+    put_out = pltpu.make_async_copy(own_t, own_out, put)
+    put_out.start()
     hand_on(4, 2 * segs - 1)
     for role in (0, 5):
         for i in range(2 * segs):
@@ -197,42 +174,83 @@
             copy.wait_send()
         else:
             pl.when(only)(copy.wait_send)
-    for copy in puts:
-        copy.wait()
-
-
-def correlate_kernel(count, place, partners, turned, win, own_scale, out, factor):
+    put_out.wait()
+
+
+def correlate_kernel(
+    count, place, partners, own_in, lag_in, win_in, out,
+    own, lag_table, wide, turned_even, turned_odd, staged, chosen, get, put,
+):
     me = place[0]
     core = lax.rem(me, 2)
     side = lax.rem(me // 2, 2)
     offsets = (1 - 2 * core, 2 - 4 * side, -4, 4, 4 * side - 2, 2 * core - 1)
-    channels = win.shape[3]
-
-    @pl.when(pl.program_id(0) == 0)
-    def _():
-        for role in range(ROLES):
-            total = jnp.zeros((8, channels), jnp.float32)
-            for seg in range(SEG):
-                rows = win[role, seg].astype(jnp.float32)
-                total += jnp.sum((rows * rows).reshape(-1, 8, channels), axis=0)
-            mean = jnp.sum(total, axis=0, keepdims=True) / (SEG * NB)
-            factor[role] = own_scale[...] * lax.rsqrt(mean + 1e-06)
-
-    def role_of(r):
+    lag_count, channels = lag_table.shape[0], own.shape[1]
+    groups = lag_count // GROUP
+
+    gets = [
+        pltpu.make_async_copy(own_in, own, get.at[ROUNDS]),
+        pltpu.make_async_copy(lag_in.at[pl.ds(place[1] * lag_count, lag_count)], lag_table, get.at[ROUNDS + 1]),
+    ]
+    for r in range(ROUNDS):
         delta = lax.rem(partners[r] - me + count + count // 2, count) - count // 2
         role = jnp.int32(0)
         for position, offset in enumerate(offsets):
             role = role + jnp.where(delta == offset, position, 0)
-        return role
-
-    left = jnp.concatenate([turned[seg] for seg in range(SEG)], axis=1)
-    for r in range(0, ROUNDS, 2):
-        roles = (role_of(r), role_of(r + 1))
-        chosen = jnp.concatenate([win[role].reshape(-1, channels) for role in roles], axis=1)
-        sums = jnp.dot(left, chosen, preferred_element_type=jnp.float32)
-        for k in range(2):
-            part = sums[:, k * channels:(k + 1) * channels].reshape(GROUP, channels, channels)
-            out[r + k] = part * factor[roles[k]][None]
+        gets.append(pltpu.make_async_copy(win_in.at[role], chosen.at[r], get.at[r]))
+    for copy in gets:
+        copy.start()
+
+    def turn(g, segments):
+        turned = (turned_even, turned_odd)[g % 2]
+        for l in range(GROUP):
+            pair = lag_table[g * GROUP + l]
+            cos, sin = pair[0:1], pair[1:2]
+            rows = slice(l * channels, (l + 1) * channels)
+            for seg in segments:
+                at = 2 * seg * NB
+                re, im = wide[seg, :, :NB], wide[seg, :, NB:]
+                turned[rows, at:at + NB] = (re * cos - im * sin).astype(jnp.bfloat16)
+                turned[rows, at + NB:at + 2 * NB] = (re * sin + im * cos).astype(jnp.bfloat16)
+
+    gets[0].wait()
+    gets[1].wait()
+    total = jnp.zeros((channels, 2 * NB), jnp.float32)
+    for seg in range(SEG):
+        values = own[seg].astype(jnp.float32)
+        wide[seg] = values
+        total += values * values
+    own_mean = jnp.sum(total, axis=1, keepdims=True) / (SEG * NB)
+    own_scale = lax.rsqrt(own_mean + 1e-06) * (1.0 / math.sqrt(SEG * NB))
+    turn(0, range(SEG))
+
+    scales = []
+    for r in range(ROUNDS):
+        gets[2 + r].wait()
+        squares = jnp.zeros((8, channels), jnp.float32)
+        for seg in range(SEG):
+            rows = chosen[r, seg].astype(jnp.float32)
+            squares += jnp.sum((rows * rows).reshape(-1, 8, channels), axis=0)
+        mean = jnp.sum(squares, axis=0, keepdims=True) / (SEG * NB)
+        scales.append(own_scale * lax.rsqrt(mean + 1e-06))
+
+    puts = []
+    for g in range(groups):
+        turned = (turned_even, turned_odd)[g % 2]
+        lags = pl.ds(g * GROUP, GROUP)
+        for r in range(0, ROUNDS, 2):
+            right = jnp.concatenate([chosen[r + k].reshape(-1, channels) for k in range(2)], axis=1)
+            sums = jnp.dot(turned[...], right, preferred_element_type=jnp.float32)
+            if g + 1 < groups:
+                turn(g + 1, (r, r + 1))
+            for k in range(2):
+                part = sums[:, k * channels:(k + 1) * channels].reshape(GROUP, channels, channels)
+                staged[r + k, lags] = part * scales[r + k][None]
+                copy = pltpu.make_async_copy(staged.at[r + k, lags], out.at[r + k, lags], put.at[len(puts)])
+                copy.start()
+                puts.append(copy)
+    for copy in puts:
+        copy.wait()
 
 
 def local(records, band_taps, white_taps, live_mask, partners):
@@ -249,38 +267,35 @@
     lag_table = np.stack(rotation(lags[:, None] * bins[None, :], samples), axis=1)
     f32 = lambda a: jnp.asarray(a.astype(np.float32))
     operands = (
-        records, jnp.asarray(table), f32(band_table), f32(white_table), f32(lag_table),
+        records, jnp.asarray(table), f32(band_table), f32(white_table),
         band_taps.reshape(1, -1), white_taps, live_mask.reshape(1, -1),
     )
 
     hbm = pl.BlockSpec(memory_space=pltpu.HBM)
     smem = pl.BlockSpec(memory_space=SMEM)
-    win, turned, own_scale = pl.pallas_call(
+    win, own_t = pl.pallas_call(
         functools.partial(gather_kernel, count, segs),
         out_shape=(
             jax.ShapeDtypeStruct((ROLES, SEG, 2 * NB, channels), jnp.bfloat16),
-            jax.ShapeDtypeStruct((SEG, lag_count * channels, 2 * NB), jnp.bfloat16),
-            jax.ShapeDtypeStruct((channels, channels), jnp.float32),
+            jax.ShapeDtypeStruct((SEG, channels, 2 * NB), jnp.bfloat16),
         ),
         in_specs=[hbm] * len(operands),
-        out_specs=(hbm, hbm, hbm),
+        out_specs=(hbm, hbm),
         scratch_shapes=[
             VMEM((SEG, 2 * NB, channels), jnp.bfloat16),
-            VMEM((SEG, lag_count * channels, 2 * NB), jnp.bfloat16),
-            VMEM((channels, channels), jnp.float32),
+            VMEM((SEG, channels, 2 * NB), jnp.bfloat16),
             VMEM(records.shape, jnp.bfloat16),
             VMEM(table.shape, jnp.bfloat16),
             VMEM(band_table.shape, jnp.float32),
             VMEM(white_table.shape, jnp.float32),
-            VMEM((lag_count, 2, NB), jnp.float32),
             VMEM((1, band_taps.shape[0]), jnp.float32),
             VMEM(white_taps.shape, jnp.float32),
             VMEM((1, channels), jnp.int32),
-            pltpu.SemaphoreType.DMA((7 + segs,)),
+            pltpu.SemaphoreType.DMA((6 + segs,)),
             pltpu.SemaphoreType.DMA((segs + 8 * SEG,)),
             pltpu.SemaphoreType.DMA((segs,)),
             pltpu.SemaphoreType.DMA((ROLES, SEG)),
-            pltpu.SemaphoreType.DMA((SEG + 1,)),
+            pltpu.SemaphoreType.DMA,
         ],
         compiler_params=pltpu.CompilerParams(
             collective_id=0, has_side_effects=True, vmem_limit_bytes=WHOLE_VMEM
@@ -288,22 +303,28 @@
         name="spectra_gather",
     )(*operands)
 
-    place = lax.axis_index("chan").astype(jnp.int32).reshape(1)
+    place = jnp.stack([lax.axis_index("chan"), lax.axis_index("tm")]).astype(jnp.int32)
+    shape = (ROUNDS, lag_count, channels, channels)
+    inner = SEG * 2 * NB
     return pl.pallas_call(
         functools.partial(correlate_kernel, count),
-        grid=(lag_count // GROUP,),
-        out_shape=jax.ShapeDtypeStruct((ROUNDS, lag_count, channels, channels), jnp.float32),
-        in_specs=[
-            smem, smem,
-            pl.BlockSpec((SEG, GROUP * channels, 2 * NB), lambda i: (0, i, 0)),
-            pl.BlockSpec(win.shape, lambda i: (0, 0, 0, 0)),
-            pl.BlockSpec(own_scale.shape, lambda i: (0, 0)),
+        out_shape=jax.ShapeDtypeStruct(shape, jnp.float32),
+        in_specs=[smem, smem, hbm, hbm, hbm],
+        out_specs=hbm,
+        scratch_shapes=[
+            VMEM((SEG, channels, 2 * NB), jnp.bfloat16),
+            VMEM((lag_count, 2, NB), jnp.float32),
+            VMEM((SEG, channels, 2 * NB), jnp.float32),
+            VMEM((GROUP * channels, inner), jnp.bfloat16),
+            VMEM((GROUP * channels, inner), jnp.bfloat16),
+            VMEM(shape, jnp.float32),
+            VMEM((ROUNDS, SEG, 2 * NB, channels), jnp.bfloat16),
+            pltpu.SemaphoreType.DMA((ROUNDS + 2,)),
+            pltpu.SemaphoreType.DMA((ROUNDS * lag_count // GROUP,)),
         ],
-        out_specs=pl.BlockSpec((ROUNDS, GROUP, channels, channels), lambda i: (0, i, 0, 0)),
-        scratch_shapes=[VMEM((ROLES, channels, channels), jnp.float32)],
         compiler_params=pltpu.CompilerParams(vmem_limit_bytes=WHOLE_VMEM),
         name="correlate",
-    )(place, partners.reshape(-1), turned, win, own_scale)
+    )(place, partners.reshape(-1), own_t, f32(lag_table), win)
 
 
 def solution(mesh):

time: 37.5 us -> 37 us (0.987)
  Pallas kernels: 37.3 us -> 36.2 us
  other arithmetic: 0 us -> 0.59 us
    pallas_call x1, Pallas kernels: 27.1 us -> 26.2 us  [local(): pl.pallas_call(functools.partial(gather_kernel, count, segs), out_shape=(...]
    another operation x0 -> x1, other arithmetic: none -> 0.59 us  [local(): jnp.stack([lax.axis_index('chan'), lax.axis_index('tm')]).astype(jnp.int32)]
where the time goes in v6:
time: 37 us; the launch traced here: 36.8 us
  Pallas kernels  36.2 us (98%)
  other arithmetic  0.59 us (2%)
    pallas_call x1, Pallas kernels, local(): pl.pallas_call(functools.partial(gather_kernel, count, segs), out_shape=(...  26.2 us
    pallas_call x1, Pallas kernels, local(): pl.pallas_call(functools.partial(correlate_kernel, count), out_shape=jax....  10 us

profile of v6, /device:TPU:0, one launch (start us, length us, event | category | flops | bytes accessed | tf_op | source)
XLA Modules:
  0.0 36.8 jit_solution(11862495957709649491)
XLA Ops:
  0.0 0.6 %pad_add_fusion.place = s32[2]{0:T(128)} fusion(s32[1]{0:T(128)} %bitcast.1, s32[1]{0:T(128)} %bitcast), kind=kLoop, calls=%fused_computation | loop fusion | flops 2 | bytes 16 | tf_op jit(solution)/shard_map/stack | solution.py:306
  0.6 26.2 %spectra_gather.1 = (bf16[6,6,256,128]{3,2,1,0:T(8,128)(2,1)}, bf16[6,128,256]{2,1,0:T(8,128)(2,1)}) custom-call(bf16[3,2048,128]{2,1,0:T(8,128)(2,1)} %rec_in.1, bf16[256,512]{1,0:T(8,128)(2,1)} %constant.16.clone.table_in, f32[128,128]{1,0:T(8,128)} %constant.17.clone.band_table_in, f32[256,16]{1,0:T(8,128)} %constant.18.clone.white_table_in, ...), custom_call_target="tpu_custom_call" | custom-call | tf_op jit(solution)/shard_map/spectra_gather/pallas_call | solution.py:276
  26.8 10.0 %correlate.1 = f32[6,16,128,128]{3,2,1,0:T(8,128)} custom-call(s32[2]{0:T(128)} %pad_add_fusion.place, s32[6]{0:T(128)} %bitcast.7, bf16[6,128,256]{2,1,0:T(8,128)(2,1)} %get-tuple-element.7.own_in, f32[32,2,128]{2,1,0:T(2,128)} %constant.19.clone.lag_in, bf16[6,6,256,128]{3,2,1,0:T(8,128)(2,1)} %get-tuple-element.8.win_in), custom_call_target="tpu_custom_call" | custom-call | tf_op jit(solution)/shard_map/correlate/pallas_call | solution.py:309

commit v7 on v4

--- a/solution.py
+++ b/solution.py
@@ -93,13 +93,17 @@
     def send_win(src, role, seg, peer, only=None):
         start(src, win.at[role, seg], recv_w.at[role, seg], peer, only)
 
+    soon_peer, late_peer = jnp.where(side == 0, down, up), jnp.where(side == 0, up, down)
+    soon_end = jnp.where(side == 0, me >= 4, me < count - 4)
+    late_end = jnp.where(side == 0, me < count - 4, me >= 4)
+
     def spread(i):
         seg = seg_at(i)
         second = i >= segs
-        send_win(own.at[seg], 2, seg, (up, tm), jnp.logical_not(last_row) if second else None)
-        send_win(own.at[seg], 3, seg, (down, tm), jnp.logical_not(first_row) if second else None)
+        send_win(own.at[seg], relay_src, seg, (soon_peer, tm), soon_end if second else None)
         if not second:
             send_win(own.at[seg], 1, seg, (across, tm))
+        send_win(own.at[seg], 2 + side, seg, (late_peer, tm), late_end if second else None)
         send_win(own.at[seg], 0, seg, (sib, tm))
 
     def relay(i):
@@ -201,38 +205,68 @@
         copy.wait()
 
 
-def correlate_kernel(count, place, partners, turned, win, own_scale, out, factor):
+def correlate_kernel(
+    count, place, partners, turned_in, win_in, scale_in, out,
+    own_scale, turned, staged, chosen, get, get_turned, put,
+):
     me = place[0]
     core = lax.rem(me, 2)
     side = lax.rem(me // 2, 2)
     offsets = (1 - 2 * core, 2 - 4 * side, -4, 4, 4 * side - 2, 2 * core - 1)
-    channels = win.shape[3]
-
-    @pl.when(pl.program_id(0) == 0)
-    def _():
-        for role in range(ROLES):
-            total = jnp.zeros((8, channels), jnp.float32)
-            for seg in range(SEG):
-                rows = win[role, seg].astype(jnp.float32)
-                total += jnp.sum((rows * rows).reshape(-1, 8, channels), axis=0)
-            mean = jnp.sum(total, axis=0, keepdims=True) / (SEG * NB)
-            factor[role] = own_scale[...] * lax.rsqrt(mean + 1e-06)
-
-    def role_of(r):
+    channels = chosen.shape[3]
+    groups = turned.shape[1] // (GROUP * channels)
+    spans = [pl.ds(g * GROUP * channels, GROUP * channels) for g in range(groups)]
+
+    gets = []
+    for r in range(ROUNDS):
         delta = lax.rem(partners[r] - me + count + count // 2, count) - count // 2
         role = jnp.int32(0)
         for position, offset in enumerate(offsets):
             role = role + jnp.where(delta == offset, position, 0)
-        return role
-
-    left = jnp.concatenate([turned[seg] for seg in range(SEG)], axis=1)
-    for r in range(0, ROUNDS, 2):
-        roles = (role_of(r), role_of(r + 1))
-        chosen = jnp.concatenate([win[role].reshape(-1, channels) for role in roles], axis=1)
-        sums = jnp.dot(left, chosen, preferred_element_type=jnp.float32)
-        for k in range(2):
-            part = sums[:, k * channels:(k + 1) * channels].reshape(GROUP, channels, channels)
-            out[r + k] = part * factor[roles[k]][None]
+        gets.append(pltpu.make_async_copy(win_in.at[role], chosen.at[r], get.at[r]))
+    gets.append(pltpu.make_async_copy(scale_in, own_scale, get.at[ROUNDS]))
+    gets_turned = [
+        pltpu.make_async_copy(turned_in.at[:, span], turned.at[:, span], get_turned.at[g])
+        for g, span in enumerate(spans)
+    ]
+    for copy in (gets[0], gets[1], gets_turned[0], gets[ROUNDS], *gets[2:ROUNDS]):
+        copy.start()
+
+    def scale(r):
+        squares = jnp.zeros((8, channels), jnp.float32)
+        for seg in range(SEG):
+            rows = chosen[r, seg].astype(jnp.float32)
+            squares += jnp.sum((rows * rows).reshape(-1, 8, channels), axis=0)
+        mean = jnp.sum(squares, axis=0, keepdims=True) / (SEG * NB)
+        return own_scale[...] * lax.rsqrt(mean + 1e-06)
+
+    scales, puts = [], []
+    for g, span in enumerate(spans):
+        lags = pl.ds(g * GROUP, GROUP)
+        for r in range(0, ROUNDS, 2):
+            if g == 0:
+                gets[r].wait()
+                gets[r + 1].wait()
+                if r == 0:
+                    gets[ROUNDS].wait()
+            if r == 0:
+                gets_turned[g].wait()
+                for ahead in ((1, 2) if g == 0 else (g + 2,)):
+                    if ahead < groups:
+                        gets_turned[ahead].start()
+            left = jnp.concatenate([turned[seg, span, :] for seg in range(SEG)], axis=1)
+            right = jnp.concatenate([chosen[r + k].reshape(-1, channels) for k in range(2)], axis=1)
+            sums = jnp.dot(left, right, preferred_element_type=jnp.float32)
+            if g == 0:
+                scales += [scale(r), scale(r + 1)]
+            for k in range(2):
+                part = sums[:, k * channels:(k + 1) * channels].reshape(GROUP, channels, channels)
+                staged[r + k, lags] = part * scales[r + k][None]
+                copy = pltpu.make_async_copy(staged.at[r + k, lags], out.at[r + k, lags], put.at[len(puts)])
+                copy.start()
+                puts.append(copy)
+    for copy in puts:
+        copy.wait()
 
 
 def local(records, band_taps, white_taps, live_mask, partners):
@@ -289,18 +323,21 @@
     )(*operands)
 
     place = lax.axis_index("chan").astype(jnp.int32).reshape(1)
+    shape = (ROUNDS, lag_count, channels, channels)
     return pl.pallas_call(
         functools.partial(correlate_kernel, count),
-        grid=(lag_count // GROUP,),
-        out_shape=jax.ShapeDtypeStruct((ROUNDS, lag_count, channels, channels), jnp.float32),
-        in_specs=[
-            smem, smem,
-            pl.BlockSpec((SEG, GROUP * channels, 2 * NB), lambda i: (0, i, 0)),
-            pl.BlockSpec(win.shape, lambda i: (0, 0, 0, 0)),
-            pl.BlockSpec(own_scale.shape, lambda i: (0, 0)),
+        out_shape=jax.ShapeDtypeStruct(shape, jnp.float32),
+        in_specs=[smem, smem, hbm, hbm, hbm],
+        out_specs=hbm,
+        scratch_shapes=[
+            VMEM(own_scale.shape, jnp.float32),
+            VMEM(turned.shape, jnp.bfloat16),
+            VMEM(shape, jnp.float32),
+            VMEM(win.shape, jnp.bfloat16),
+            pltpu.SemaphoreType.DMA((ROUNDS + 1,)),
+            pltpu.SemaphoreType.DMA((lag_count // GROUP,)),
+            pltpu.SemaphoreType.DMA((ROUNDS * lag_count // GROUP,)),
         ],
-        out_specs=pl.BlockSpec((ROUNDS, GROUP, channels, channels), lambda i: (0, i, 0, 0)),
-        scratch_shapes=[VMEM((ROLES, channels, channels), jnp.float32)],
         compiler_params=pltpu.CompilerParams(vmem_limit_bytes=WHOLE_VMEM),
         name="correlate",
     )(place, partners.reshape(-1), turned, win, own_scale)

time: 37.5 us -> 39.5 us (1.053)
  Pallas kernels: 37.3 us -> 39.3 us
    pallas_call x1, Pallas kernels: 10.3 us -> 12.3 us  [local(): pl.pallas_call(functools.partial(correlate_kernel, count), out_shape=jax....]
where the time goes in v7:
time: 39.5 us; the launch traced here: 39.3 us
  Pallas kernels  39.3 us (99%)
    pallas_call x1, Pallas kernels, local(): pl.pallas_call(functools.partial(gather_kernel, count, segs), out_shape=(...  27.1 us
    pallas_call x1, Pallas kernels, local(): pl.pallas_call(functools.partial(correlate_kernel, count), out_shape=jax....  12.3 us

profile of v7, /device:TPU:0, one launch (start us, length us, event | category | flops | bytes accessed | tf_op | source)
XLA Modules:
  0.0 39.3 jit_solution(9880715884706766210)
XLA Ops:
  0.0 27.1 %spectra_gather.1 = (bf16[6,6,256,128]{3,2,1,0:T(8,128)(2,1)}, bf16[6,2048,256]{2,1,0:T(8,128)(2,1)}, f32[128,128]{1,0:T(8,128)}) custom-call(bf16[3,2048,128]{2,1,0:T(8,128)(2,1)} %rec_in.1, bf16[256,512]{1,0:T(8,128)(2,1)} %constant.14.clone.table_in, f32[128,128]{1,0:T(8,128)} %constant.15.clone.band_table_in, f32[256,16]{1,0:T(8,128)} %constant.16.clone.white_table_in, ...), custom_call_target="tpu_custom_call" | custom-call | tf_op jit(solution)/shard_map/spectra_gather/pallas_call | solution.py:292
  27.1 12.3 %correlate.1 = f32[6,16,128,128]{3,2,1,0:T(8,128)} custom-call(s32[1]{0:T(128)} %bitcast.place, s32[6]{0:T(128)} %bitcast.6, bf16[6,2048,256]{2,1,0:T(8,128)(2,1)} %get-tuple-element.8.turned_in, bf16[6,6,256,128]{3,2,1,0:T(8,128)(2,1)} %get-tuple-element.9.win_in, f32[128,128]{1,0:T(8,128)} %get-tuple-element.10.scale_in), custom_call_target="tpu_custom_call" | custom-call | tf_op jit(solution)/shard_map/correlate/pallas_call | solution.py:327

commit v8 on v6

--- a/solution.py
+++ b/solution.py
@@ -178,10 +178,10 @@
 
 
 def correlate_kernel(
-    count, place, partners, own_in, lag_in, win_in, out,
+    count, chan_at, tm_at, partners, own_in, lag_in, win_in, out,
     own, lag_table, wide, turned_even, turned_odd, staged, chosen, get, put,
 ):
-    me = place[0]
+    me = chan_at[0]
     core = lax.rem(me, 2)
     side = lax.rem(me // 2, 2)
     offsets = (1 - 2 * core, 2 - 4 * side, -4, 4, 4 * side - 2, 2 * core - 1)
@@ -190,7 +190,7 @@
 
     gets = [
         pltpu.make_async_copy(own_in, own, get.at[ROUNDS]),
-        pltpu.make_async_copy(lag_in.at[pl.ds(place[1] * lag_count, lag_count)], lag_table, get.at[ROUNDS + 1]),
+        pltpu.make_async_copy(lag_in.at[pl.ds(tm_at[0] * lag_count, lag_count)], lag_table, get.at[ROUNDS + 1]),
     ]
     for r in range(ROUNDS):
         delta = lax.rem(partners[r] - me + count + count // 2, count) - count // 2
@@ -303,13 +303,13 @@
         name="spectra_gather",
     )(*operands)
 
-    place = jnp.stack([lax.axis_index("chan"), lax.axis_index("tm")]).astype(jnp.int32)
+    chan_at, tm_at = (lax.axis_index(axis).astype(jnp.int32).reshape(1) for axis in ("chan", "tm"))
     shape = (ROUNDS, lag_count, channels, channels)
     inner = SEG * 2 * NB
     return pl.pallas_call(
         functools.partial(correlate_kernel, count),
         out_shape=jax.ShapeDtypeStruct(shape, jnp.float32),
-        in_specs=[smem, smem, hbm, hbm, hbm],
+        in_specs=[smem, smem, smem, hbm, hbm, hbm],
         out_specs=hbm,
         scratch_shapes=[
             VMEM((SEG, channels, 2 * NB), jnp.bfloat16),
@@ -324,7 +324,7 @@
         ],
         compiler_params=pltpu.CompilerParams(vmem_limit_bytes=WHOLE_VMEM),
         name="correlate",
-    )(place, partners.reshape(-1), own_t, f32(lag_table), win)
+    )(chan_at, tm_at, partners.reshape(-1), own_t, f32(lag_table), win)
 
 
 def solution(mesh):

time: 37 us -> 36.4 us (0.984)
  other arithmetic: 0.59 us -> 0 us
    another operation x1 -> x0, other arithmetic: 0.59 us -> none  [local(): jnp.stack([lax.axis_index('chan'), lax.axis_index('tm')]).astype(jnp.int32)]
where the time goes in v8:
time: 36.4 us; the launch traced here: 36.2 us
  Pallas kernels  36.2 us (99%)
    pallas_call x1, Pallas kernels, local(): pl.pallas_call(functools.partial(gather_kernel, count, segs), out_shape=(...  26.2 us
    pallas_call x1, Pallas kernels, local(): pl.pallas_call(functools.partial(correlate_kernel, count), out_shape=jax....  10 us

profile of v8, /device:TPU:0, one launch (start us, length us, event | category | flops | bytes accessed | tf_op | source)
XLA Modules:
  0.0 36.2 jit_solution(7662845825182535418)
XLA Ops:
  0.0 26.2 %spectra_gather.1 = (bf16[6,6,256,128]{3,2,1,0:T(8,128)(2,1)}, bf16[6,128,256]{2,1,0:T(8,128)(2,1)}) custom-call(bf16[3,2048,128]{2,1,0:T(8,128)(2,1)} %rec_in.1, bf16[256,512]{1,0:T(8,128)(2,1)} %constant.16.clone.table_in, f32[128,128]{1,0:T(8,128)} %constant.17.clone.band_table_in, f32[256,16]{1,0:T(8,128)} %constant.18.clone.white_table_in, ...), custom_call_target="tpu_custom_call" | custom-call | tf_op jit(solution)/shard_map/spectra_gather/pallas_call | solution.py:276
  26.2 10.0 %correlate.1 = f32[6,16,128,128]{3,2,1,0:T(8,128)} custom-call(s32[1]{0:T(128)} %bitcast.chan_at, s32[1]{0:T(128)} %bitcast.1.tm_at, s32[6]{0:T(128)} %bitcast.7, bf16[6,128,256]{2,1,0:T(8,128)(2,1)} %get-tuple-element.7.own_in, f32[32,2,128]{2,1,0:T(2,128)} %constant.19.clone.lag_in, bf16[6,6,256,128]{3,2,1,0:T(8,128)(2,1)} %get-tuple-element.8.win_in), custom_call_target="tpu_custom_call" | custom-call | tf_op jit(solution)/shard_map/correlate/pallas_call | solution.py:309
